TPU v7x, 32 devices: a whole 2x2x4 slice. The times are simulated.
32 devices in a mesh: dp: 16 (over z, x, core), mp: 2 (over y).
Axes of the slice: x: 2, y: 2, z: 4, core: 2. Of those that a mesh axis runs over, the one named last changes fastest.
Arguments:
- session_length: int32 [16], P('dp'), may hold values from 1 to 128
- event_owner: int32 [2048, 1], P('dp'), may hold values from 0 to 15; in each aligned block of 128 rows (0 to 127, 128 to 255, ...) at most 16 rows name the same one
- event_row: int32 [2048], P('dp'), may hold values from 0 to 255
- text_rows: bfloat16 [4096, 4096], P('dp', 'mp'), may hold values from -6 to 6
- image_rows: bfloat16 [4096, 4096], P('dp', 'mp'), may hold values from -6 to 6
- price: float32 [4096], P('dp'), may hold values from 0.2 to 5
- price_dir: bfloat16 [4096], P('mp'), may hold values from -4 to 4
- norm_gain: bfloat16 [4096], P('mp'), may hold values from 0.5 to 1.5
- w_query: bfloat16 [4096, 2048], P('dp', 'mp'), may hold values from -1 to 1
- w_key: bfloat16 [4096, 2048], P('dp', 'mp'), may hold values from -1 to 1
- w_value: bfloat16 [4096, 2048], P('dp', 'mp'), may hold values from -0.09375 to 0.09375
- cotangent: bfloat16 [2048, 4096], P('dp', 'mp'), may hold values from -6 to 6
Outputs:
- context: bfloat16 [2048, 2048], P('dp', 'mp')
- text_grad: float32 [4096, 4096], P('dp', 'mp')
- image_grad: float32 [4096, 4096], P('dp', 'mp')
Inputs may be any that keep to these rules, and one draw needn't show every extreme that they name: `event_owner`: among the event slots of one index of dp, no owner is named more than 16 times, a bound that some block reaches.
All inputs are finite; a program needn't handle non-finite values.
Results may differ from a plain program's by a relative error of at most 0.0063.
Values may be sent and summed in bfloat16 or wider, within the bound.
A program may use at most 64 MiB of HBM per device.

v0:
```python
import math

import jax
import jax.numpy as jnp
from jax import lax
from jax.sharding import PartitionSpec as P

D = 4096
HD = 128
SLOT = 128


def fetch_rows(requests, text_rows, image_rows):
    row_ids = jnp.maximum(requests, 0)
    return (row_ids, text_rows[row_ids], image_rows[row_ids])


def join_rows(row_ids, text_got, image_got, price, price_dir):
    price_got = price[row_ids]
    mixed = text_got.astype(jnp.float32) * image_got.astype(jnp.float32) + price_got[
        ..., None
    ] * price_dir.astype(jnp.float32)
    return mixed.astype(jnp.bfloat16)


def answer(requests, text_rows, image_rows, price, price_dir):
    row_ids, text_got, image_got = fetch_rows(requests, text_rows, image_rows)
    joined_rows = join_rows(row_ids, text_got, image_got, price, price_dir)
    replies = lax.all_to_all(joined_rows, "dp", split_axis=0, concat_axis=0, tiled=True)
    return (replies, row_ids, text_got, image_got)


def credit_rows(row_ids, grad_rows, text_got, image_got, table_rows):
    col_width = grad_rows.shape[-1]
    flat_ids = row_ids.reshape(-1)
    grad_float = grad_rows.astype(jnp.float32)
    text_terms = (grad_float * image_got.astype(jnp.float32)).reshape(-1, col_width)
    image_terms = (grad_float * text_got.astype(jnp.float32)).reshape(-1, col_width)
    text_grad = jax.ops.segment_sum(text_terms, flat_ids, num_segments=table_rows)
    image_grad = jax.ops.segment_sum(image_terms, flat_ids, num_segments=table_rows)
    return (text_grad, image_grad)


def attend(query, keys, values, session_length):
    sessions = session_length.shape[0]
    heads_here = query.shape[1] // HD
    shape4 = (sessions, SLOT, heads_here, HD)
    scores = jnp.einsum(
        "sqhd,skhd->shqk",
        query.reshape(shape4),
        keys.reshape(shape4),
        preferred_element_type=jnp.float32,
    ) / math.sqrt(HD)
    position = jnp.arange(SLOT, dtype=jnp.int32)
    live_mask = position[None, :] < session_length[:, None]
    allowed = (position[None, :] <= position[:, None])[None, None, :, :] & live_mask[
        :, None, None, :
    ]
    scores = jnp.where(allowed, scores, jnp.float32(-1e30))
    row_max = jnp.max(scores, axis=-1, keepdims=True)
    powers = jnp.exp(scores - row_max)
    probs = (powers / jnp.sum(powers, axis=-1, keepdims=True)).astype(jnp.bfloat16)
    context = jnp.einsum(
        "shqk,skhd->sqhd", probs, values.reshape(shape4), preferred_element_type=jnp.float32
    )
    context = jnp.where(live_mask[:, :, None, None], context, jnp.float32(0.0))
    return context.reshape(sessions * SLOT, heads_here * HD).astype(jnp.bfloat16)


def local(
    session_length,
    event_owner,
    event_row,
    text_rows,
    image_rows,
    price,
    price_dir,
    norm_gain,
    w_query,
    w_key,
    w_value,
    cotangent,
):
    peers = lax.axis_size("dp")
    tok_count = event_row.shape[0]
    capacity = 2 * tok_count // peers
    col_width = text_rows.shape[1]
    table_rows = text_rows.shape[0]
    owner_ids = event_owner[:, 0]
    member = (owner_ids[:, None] == jnp.arange(peers, dtype=jnp.int32)[None, :]).astype(jnp.int32)
    earlier = jnp.sum((jnp.cumsum(member, axis=0) - member) * member, axis=1)
    slot_ids = owner_ids * capacity + earlier
    requests = (
        jnp.full((peers * capacity,), -1, jnp.int32)
        .at[slot_ids]
        .set(event_row)
        .reshape(peers, capacity)
    )
    grad_buffer = (
        jnp.zeros((peers * capacity, col_width), jnp.bfloat16)
        .at[slot_ids]
        .set(cotangent)
        .reshape(peers, capacity, col_width)
    )
    replies = answer(
        lax.all_to_all(requests, "dp", split_axis=0, concat_axis=0, tiled=True),
        text_rows,
        image_rows,
        price,
        price_dir,
    )[0]
    got_ids, got_grads = (
        lax.all_to_all(requests, "dp", split_axis=0, concat_axis=0, tiled=True),
        lax.all_to_all(grad_buffer, "dp", split_axis=0, concat_axis=0, tiled=True),
    )
    row_ids, text_got, image_got = fetch_rows(got_ids, text_rows, image_rows)
    text_grad, image_grad = credit_rows(row_ids, got_grads, text_got, image_got, table_rows)
    joined_rows = replies.reshape(peers * capacity, col_width)[slot_ids]
    joined_float = joined_rows.astype(jnp.float32)
    square_sums = lax.psum(jnp.sum(joined_float * joined_float, axis=1), "mp")
    scale = lax.rsqrt(square_sums / D + 1e-06)
    normed = (joined_float * scale[:, None] * norm_gain.astype(jnp.float32)[None, :]).astype(
        jnp.bfloat16
    )
    features_all = lax.all_gather(normed, "mp", axis=1, tiled=True)

    def add_rows(weight_rows):
        return jnp.dot(features_all, weight_rows, preferred_element_type=jnp.float32)

    query_sum = add_rows(lax.all_gather(w_query, "dp", axis=0, tiled=True))
    key_sum = add_rows(lax.all_gather(w_key, "dp", axis=0, tiled=True))
    value_sum = add_rows(lax.all_gather(w_value, "dp", axis=0, tiled=True))
    context = attend(
        query_sum.astype(jnp.bfloat16),
        key_sum.astype(jnp.bfloat16),
        value_sum.astype(jnp.bfloat16),
        session_length,
    )
    return (context, text_grad, image_grad)


def solution(mesh):
    return jax.shard_map(
        local,
        mesh=mesh,
        in_specs=(
            P("dp"),
            P("dp", None),
            P("dp"),
            P("dp", "mp"),
            P("dp", "mp"),
            P("dp"),
            P("mp"),
            P("mp"),
            P("dp", "mp"),
            P("dp", "mp"),
            P("dp", "mp"),
            P("dp", "mp"),
        ),
        out_specs=(P("dp", "mp"), P("dp", "mp"), P("dp", "mp")),
        check_vma=False,
    )
```

profile of v0, /device:TPU:0, one launch (start us, length us, event | category | flops | bytes accessed | tf_op | source)
XLA Modules:
  0.0 357.1 jit_solution(746152147235199852)
XLA Ops:
  7.2 0.8 fusion.24
  8.2 0.8 select_reduce_fusion
  9.0 0.7 fusion.26
  9.7 1.1 scatter_custom_fusion
  10.8 0.7 all_to_all.13
  11.5 7.4 %all-to-all-start = ((s32[16,1,16]{2,1,0:T(1,128)}), s32[16,1,16]{2,1,0:T(1,128)S(1)}, u32[]{:S(2)}, u32[]{:S(2)}) async-start(s32[16,1,16]{2,1,0:T(1,128)} %all_to_all.13), calls=%async_computation | async-start | bytes 16384 | tf_op jit(solution)/shard_map/all_to_all | solution.py:106
  18.9 2.9 scatter_custom_fusion.1
  21.8 3.4 all-to-all-done
  25.2 3.7 %all-to-all-start.2 = ((bf16[16,16,2048]{2,1,0:T(8,128)(2,1)}), bf16[16,16,2048]{2,1,0:T(8,128)(2,1)S(1)}, u32[]{:S(2)}, u32[]{:S(2)}) async-start(bf16[16,16,2048]{2,1,0:T(8,128)(2,1)} %bitcast.11), calls=%async_computation.2 | async-start | bytes 2097152 | tf_op jit(solution)/shard_map/all_to_all | solution.py:114
  29.0 2.3 gather_fusion
  31.4 2.3 gather_fusion.1
  33.7 1.9 gather_fusion.2
  35.7 16.0 %all-to-all-done.2 = bf16[16,16,2048]{2,1,0:T(8,128)(2,1)S(1)} async-done(((bf16[16,16,2048]{2,1,0:T(8,128)(2,1)}), bf16[16,16,2048]{2,1,0:T(8,128)(2,1)S(1)}, u32[]{:S(2)}, u32[]{:S(2)}) %all-to-all-start.2) | async-done | bytes 1048608 | tf_op jit(solution)/shard_map/all_to_all | solution.py:114
  51.8 4.3 %convert_multiply_fusion = (f32[16,16,2048]{2,1,0:T(8,128)}, f32[16,16,2048]{2,1,0:T(8,128)}, bf16[16,16,2048]{2,1,0:T(8,128)(2,1)}) fusion(bf16[16,16,2048]{2,1,0:T(8,128)(2,1)S(1)} %bitcast.47, bf16[16,16,2048]{2,1,0:T(8,128)(2,1)S(1)} %all-to-all-done.2, bf16[16,16,2048]{2,1,0:T(8,128)(2,1)} %bitcast.48, f32[2048]{0:T(1024)S(1)} %convert_element_type.54, ...), kind=kLoop, calls=%fused_computation.9 | loop fusion | flops 4718592 | bytes 8397824 | tf_op jit(solution)/shard_map/mul | solution.py:38
  56.0 6.9 %all-to-all-start.1 = ((bf16[16,16,2048]{2,1,0:T(8,128)(2,1)}), bf16[16,16,2048]{2,1,0:T(8,128)(2,1)S(1)}, u32[]{:S(2)}, u32[]{:S(2)}) async-start(bf16[16,16,2048]{2,1,0:T(8,128)(2,1)} %get-tuple-element.11), calls=%async_computation.1 | async-start | bytes 2097152 | tf_op jit(solution)/shard_map/all_to_all | solution.py:29
  63.1 22.9 %all-to-all-done.1 = bf16[16,16,2048]{2,1,0:T(8,128)(2,1)S(1)} async-done(((bf16[16,16,2048]{2,1,0:T(8,128)(2,1)}), bf16[16,16,2048]{2,1,0:T(8,128)(2,1)S(1)}, u32[]{:S(2)}, u32[]{:S(2)}) %all-to-all-start.1) | async-done | bytes 1048608 | tf_op jit(solution)/shard_map/all_to_all | solution.py:29
  85.9 0.9 gather_fusion.3
  87.1 4.9 %psum.7 = f32[128]{0:T(128)S(1)} all-reduce(f32[128]{0:T(128)S(1)} %fusion.10), channel_id=1, replica_groups=mesh['dp'=16,'mp'=2] {'mp'}, use_global_device_ids=true, to_apply=%region_4.5 | all-reduce | flops 128 | bytes 1024 | tf_op jit(solution)/shard_map/psum | solution.py:120
  92.0 1.0 fusion.12
  93.1 0.7 all-gather.7.cloned.1.call-update
  93.8 0.7 all-gather.11.cloned.1.call-update
  94.5 0.5 all-gather.9.cloned.1.call-update
  95.8 6.2 %scatter_custom_fusion.2 = f32[256,2048]{1,0:T(8,128)} fusion(s32[256]{0:T(256)S(1)} %reshape.144, f32[256,2048]{1,0:T(8,128)} %bitcast.50, f32[]{:T(128)} %constant.15.clone.1), kind=kCustom, calls=%fused_computation.33 | custom fusion | flops 524288 | bytes 2097664 | tf_op jit(solution)/shard_map/scatter-add | solution.py:39
  102.0 6.2 %scatter_custom_fusion.3 = f32[256,2048]{1,0:T(8,128)} fusion(s32[256]{0:T(256)S(1)} %reshape.144, f32[256,2048]{1,0:T(8,128)} %bitcast.49, f32[]{:T(128)} %constant.15.clone.1), kind=kCustom, calls=%fused_computation.31 | custom fusion | flops 524288 | bytes 2097664 | tf_op jit(solution)/shard_map/scatter-add | solution.py:40
  108.2 8.5 %all-gather.5.cloned.1.call-done = bf16[128,4096]{1,0:T(8,128)(2,1)} async-done(((bf16[128,2048]{1,0:T(8,128)(2,1)}), bf16[128,4096]{1,0:T(8,128)(2,1)}) %all-gather.5.cloned.1.call-update) | async-done | bytes 1048592 | tf_op jit(solution)/shard_map/all_gather | solution.py:125
  116.7 77.1 %all-gather.7.cloned.1.call-done = bf16[4096,1024]{1,0:T(8,128)(2,1)} async-done(((bf16[256,1024]{1,0:T(8,128)(2,1)}), bf16[4096,1024]{1,0:T(8,128)(2,1)}) %all-gather.7.cloned.1.call-update) | async-done | bytes 8388624 | tf_op jit(solution)/shard_map/all_gather | solution.py:132
  193.8 5.0 %convolution_convert_fusion.2 = bf16[128,1024]{1,0:T(8,128)(2,1)S(1)} fusion(bf16[128,4096]{1,0:T(8,128)(2,1)} %all-gather.5.cloned.1.call-done, bf16[4096,1024]{1,0:T(8,128)(2,1)} %all-gather.7.cloned.1.call-done), kind=kOutput, calls=%fused_computation.23 | convolution fusion | flops 1073872896 | bytes 9699328 | tf_op jit(solution)/shard_map/dot_general | solution.py:128
  198.9 70.2 %all-gather.11.cloned.1.call-done = bf16[4096,1024]{1,0:T(8,128)(2,1)} async-done(((bf16[256,1024]{1,0:T(8,128)(2,1)}), bf16[4096,1024]{1,0:T(8,128)(2,1)}) %all-gather.11.cloned.1.call-update) | async-done | bytes 8388624 | tf_op jit(solution)/shard_map/all_gather | solution.py:131
  269.1 4.6 %fusion.9 = bf16[16,8,8,128]{3,2,1,0:T(8,128)(2,1)S(1)} fusion(bf16[128,4096]{1,0:T(8,128)(2,1)S(1)} %copy-done.3, bf16[4096,1024]{1,0:T(8,128)(2,1)} %all-gather.11.cloned.1.call-done), kind=kOutput, calls=%fused_computation.27 | convolution fusion | flops 1073872896 | bytes 9699328 | tf_op jit(solution)/shard_map/dot_general | solution.py:128
  273.8 70.6 %all-gather.9.cloned.1.call-done = bf16[4096,1024]{1,0:T(8,128)(2,1)} async-done(((bf16[256,1024]{1,0:T(8,128)(2,1)}), bf16[4096,1024]{1,0:T(8,128)(2,1)}) %all-gather.9.cloned.1.call-update) | async-done | bytes 8388624 | tf_op jit(solution)/shard_map/all_gather | solution.py:130
  344.3 4.6 %fusion.8 = bf16[16,8,8,128]{3,2,1,0:T(8,128)(2,1)S(1)} fusion(bf16[128,4096]{1,0:T(8,128)(2,1)S(1)} %copy-done.3, bf16[4096,1024]{1,0:T(8,128)(2,1)} %all-gather.9.cloned.1.call-done), kind=kOutput, calls=%fused_computation.26 | convolution fusion | flops 1073872896 | bytes 9699328 | tf_op jit(solution)/shard_map/dot_general | solution.py:128
  349.7 0.9 copy.24
  (35 shorter events, 1.8 us)
Async XLA Ops:
  7.2 21.8 %copy-start = (bf16[256,2048]{1,0:T(8,128)(2,1)S(1)}, bf16[256,2048]{1,0:T(8,128)(2,1)}, u32[]{:S(2)}) copy-start(bf16[256,2048]{1,0:T(8,128)(2,1)} %param.15) | copy-start | bytes 3145732
  7.2 21.7 %copy-start.5 = (bf16[2048]{0:T(1024)(128)(2,1)S(1)}, bf16[2048]{0:T(1024)(128)(2,1)}, u32[]{:S(2)}) copy-start(bf16[2048]{0:T(1024)(128)(2,1)} %param.18) | copy-start | bytes 12292
  11.5 13.7 %all-to-all-start = ((s32[16,1,16]{2,1,0:T(1,128)}), s32[16,1,16]{2,1,0:T(1,128)S(1)}, u32[]{:S(2)}, u32[]{:S(2)}) async-start(s32[16,1,16]{2,1,0:T(1,128)} %all_to_all.13), calls=%async_computation | async-start | bytes 16384 | tf_op jit(solution)/shard_map/all_to_all | solution.py:106
  25.2 26.6 %all-to-all-start.2 = ((bf16[16,16,2048]{2,1,0:T(8,128)(2,1)}), bf16[16,16,2048]{2,1,0:T(8,128)(2,1)S(1)}, u32[]{:S(2)}, u32[]{:S(2)}) async-start(bf16[16,16,2048]{2,1,0:T(8,128)(2,1)} %bitcast.11), calls=%async_computation.2 | async-start | bytes 2097152 | tf_op jit(solution)/shard_map/all_to_all | solution.py:114
  29.0 2.3 copy-start.2
  31.4 2.4 copy-start.1
  33.7 18.0 %copy-start.4 = (bf16[256,2048]{1,0:T(8,128)(2,1)S(1)}, bf16[256,2048]{1,0:T(8,128)(2,1)}, u32[]{:S(2)}) copy-start(bf16[256,2048]{1,0:T(8,128)(2,1)} %gather_fusion) | copy-start | bytes 3145732
  56.0 7.0 %copy-start.6 = (bf16[2048]{0:T(1024)(128)(2,1)S(1)}, bf16[2048]{0:T(1024)(128)(2,1)}, u32[]{:S(2)}) copy-start(bf16[2048]{0:T(1024)(128)(2,1)} %param.19) | copy-start | bytes 12292
  56.0 29.9 %all-to-all-start.1 = ((bf16[16,16,2048]{2,1,0:T(8,128)(2,1)}), bf16[16,16,2048]{2,1,0:T(8,128)(2,1)S(1)}, u32[]{:S(2)}, u32[]{:S(2)}) async-start(bf16[16,16,2048]{2,1,0:T(8,128)(2,1)} %get-tuple-element.11), calls=%async_computation.1 | async-start | bytes 2097152 | tf_op jit(solution)/shard_map/all_to_all | solution.py:29
  63.0 53.7 %all-gather.5.cloned.1.call-start = ((), (), s32[]{:S(2)}) async-start(), calls=%async_computation.3 | async-start | bytes 1572864 | tf_op jit(solution)/shard_map/all_gather | solution.py:125
  93.0 100.8 %all-gather.7.cloned.1.call-start = ((), (), s32[]{:S(2)}) async-start(), calls=%async_computation.4 | async-start | bytes 8912896 | tf_op jit(solution)/shard_map/all_gather | solution.py:132
  93.8 175.4 %all-gather.11.cloned.1.call-start = ((), (), s32[]{:S(2)}) async-start(), calls=%async_computation.6 | async-start | bytes 8912896 | tf_op jit(solution)/shard_map/all_gather | solution.py:131
  94.5 249.8 %all-gather.9.cloned.1.call-start = ((), (), s32[]{:S(2)}) async-start(), calls=%async_computation.5 | async-start | bytes 8912896 | tf_op jit(solution)/shard_map/all_gather | solution.py:130
  116.7 152.4 %copy-start.3 = (bf16[128,4096]{1,0:T(8,128)(2,1)S(1)}, bf16[128,4096]{1,0:T(8,128)(2,1)}, u32[]{:S(2)}) copy-start(bf16[128,4096]{1,0:T(8,128)(2,1)} %all-gather.5.cloned.1.call-done) | copy-start | bytes 3145732
Sparse Core Ops, SparseCore 0:
  93.1 23.5 all-gather.4
  118.8 74.8 all-gather.6
  195.9 73.1 all-gather.10
  271.1 73.1 all-gather.8
where the time goes:
time: 358 us; the launch traced here: 357 us
  waiting for transfers between devices  270 us (75%)
  other arithmetic  20.6 us (6%)
  starting transfers between devices  18.1 us (5%)
  matrix products  14.8 us (4%)
  between operations  14.6 us (4%)
  local copies, waits for them, and re-layouts  13.5 us (4%)
  blocking collectives  4.93 us (1%)
    all_gather x1, waiting for transfers between devices, local(): value_sum = add_rows(lax.all_gather(w_value, 'dp', axis=0, tiled=True))  77.1 us
    all_gather x1, waiting for transfers between devices, local(): query_sum = add_rows(lax.all_gather(w_query, 'dp', axis=0, tiled=True))  70.6 us
    all_gather x1, waiting for transfers between devices, local(): key_sum = add_rows(lax.all_gather(w_key, 'dp', axis=0, tiled=True))  70.2 us
    all_to_all x1, waiting for transfers between devices, answer(): lax.all_to_all(joined_rows, 'dp', split_axis=0, concat_axis=0, tiled=True)  22.9 us
    all_to_all x1, waiting for transfers between devices, local(): lax.all_to_all(grad_buffer, 'dp', split_axis=0, concat_axis=0, tiled=True)  16 us
    dot_general x3, matrix products, add_rows(): jnp.dot(features_all, weight_rows, preferred_element_type=jnp.float32)  14.2 us
    all_gather x1, waiting for transfers between devices, local(): features_all = lax.all_gather(normed, 'mp', axis=1, tiled=True)  8.49 us
    all_to_all x1, starting transfers between devices, local(): lax.all_to_all(requests, 'dp', split_axis=0, concat_axis=0, tiled=True)  7.36 us
  transfers between devices with their start and end apart: 7, of which 7 were waited for; matrix products, arithmetic and copies ran while one was open for 9% of the time, Pallas kernels for 0%

commit v1 on v0

--- a/solution.py
+++ b/solution.py
@@ -3,6 +3,8 @@
 import jax
 import jax.numpy as jnp
 from jax import lax
+from jax.experimental import pallas as pl
+from jax.experimental.pallas import tpu as pltpu
 from jax.sharding import PartitionSpec as P
 
 D = 4096
@@ -67,7 +69,7 @@
     return context.reshape(sessions * SLOT, heads_here * HD).astype(jnp.bfloat16)
 
 
-def local(
+def local_any(
     session_length,
     event_owner,
     event_row,
@@ -139,9 +141,348 @@
     return (context, text_grad, image_grad)
 
 
+def flip(index, bit):
+    return index + bit - 2 * bit * ((index // bit) % 2)
+
+
+def exchange_kernel(
+    reqs_ref, small_ref, price_ref, dir_ref, gain_ref, text_ref, image_ref, cot_ref,
+    wq_ref, wk_ref, wv_ref,
+    ctx_ref, gsum_ref,
+    ids, rep_out, rep_in, grad_out, grad_in, wbuf, xfull, xpart, xown, xsend, part_own,
+    part_out, part_in,
+    load_sem, id_s, id_r, rep_s, rep_r, grad_s, grad_r, w_s, w_r, y_s, y_r, x_s, x_r, p_s, p_r,
+):
+    me = lax.axis_index("dp")
+    my_y = lax.axis_index("mp")
+    n = 16
+    cap = 16
+    rel = me % 8
+    half = me // 8
+    wrows = wq_ref.shape[0]
+    qw = wq_ref.shape[1]
+    loads = [
+        pltpu.make_async_copy(w, wbuf.at[k, pl.ds(rel * wrows, wrows), :], load_sem.at[k])
+        for k, w in enumerate((wq_ref, wk_ref, wv_ref))
+    ]
+    for load in loads:
+        load.start()
+    barrier = pltpu.get_barrier_semaphore()
+
+    def greet(i, carry):
+        pl.semaphore_signal(
+            barrier, inc=1, device_id={"dp": (me + i) % n}, device_id_type=pl.DeviceIdType.MESH
+        )
+        return carry
+
+    lax.fori_loop(1, n, greet, 0)
+    pl.semaphore_signal(
+        barrier, inc=1, device_id={"mp": 1 - my_y}, device_id_type=pl.DeviceIdType.MESH
+    )
+    pl.semaphore_wait(barrier, n)
+
+    def remote(src, dst, send, recv, **to):
+        return pltpu.make_async_remote_copy(
+            src_ref=src, dst_ref=dst, send_sem=send, recv_sem=recv, device_id=to,
+            device_id_type=pl.DeviceIdType.MESH,
+        )
+
+    def swap(src, dst, send, recv):
+        def one(i):
+            peer = (me + i) % n
+            return remote(
+                src.at[pl.ds(peer * cap, cap), :], dst.at[pl.ds(me * cap, cap), :],
+                send.at[i], recv.at[i], dp=peer,
+            )
+
+        def start(i, carry):
+            one(i).start()
+            return carry
+
+        def finish(i, carry):
+            one(i).wait_send()
+            one(i).wait_recv()
+            return carry
+
+        return (
+            lambda: lax.fori_loop(1, n, start, 0),
+            lambda: lax.fori_loop(1, n, finish, 0),
+        )
+
+    mine = pl.ds(me * cap, cap)
+    id_start, id_finish = swap(reqs_ref, ids, id_s, id_r)
+    id_start()
+    ids[mine, :] = reqs_ref[mine, :]
+
+    def shard(rel_index, low=0, count=wrows):
+        return wbuf.at[:, pl.ds(rel_index * wrows + low, count), :]
+
+    def send_w(k, rel_index, bit, low=0, count=wrows):
+        block = shard(rel_index, low, count)
+        return remote(block, block, w_s.at[k], w_r.at[k], dp=flip(me, bit))
+
+    for load in loads:
+        load.wait()
+    own_x, own_z, own_c = send_w(0, rel, 2), send_w(1, rel, 4), send_w(2, rel, 1)
+    own_x.start()
+    own_z.start()
+    own_c.start()
+
+    slot = small_ref[0:1, :]
+    pick = (
+        lax.broadcasted_iota(jnp.int32, (n * cap, SLOT), 0) == slot
+    ).astype(jnp.float32).astype(jnp.bfloat16)
+    tile = 512
+    tiles = text_ref.shape[1] // tile
+
+    def column(j):
+        return pl.ds(pl.multiple_of(j * tile, tile), tile)
+
+    def pack_grads(j, carry):
+        at = column(j)
+        grad_out[:, at] = jnp.dot(
+            pick, cot_ref[:, at], preferred_element_type=jnp.float32
+        ).astype(jnp.bfloat16)
+        return carry
+
+    lax.fori_loop(0, tiles, pack_grads, 0)
+    id_finish()
+    got = ids[...]
+    lane = lax.broadcasted_iota(jnp.int32, got.shape, 1)
+    table = text_ref.shape[0]
+    want = jnp.concatenate(
+        [(got == lane + 128 * k).astype(jnp.float32) for k in range(table // 128)], axis=1
+    ).astype(jnp.bfloat16)
+    price = price_ref[...]
+
+    def reply(j, carry):
+        at = column(j)
+        mixed = text_ref[:, at].astype(jnp.float32) * image_ref[:, at].astype(
+            jnp.float32
+        ) + price * dir_ref[:, at].astype(jnp.float32)
+        rep_out[:, at] = jnp.dot(
+            want, mixed.astype(jnp.bfloat16), preferred_element_type=jnp.float32
+        ).astype(jnp.bfloat16)
+        return carry
+
+    lax.fori_loop(0, tiles, reply, 0)
+    rep_start, rep_finish = swap(rep_out, rep_in, rep_s, rep_r)
+    rep_start()
+    rep_in[mine, :] = rep_out[mine, :]
+    rep_finish()
+
+    def unpack(j, carry):
+        at = column(j)
+        xfull[my_y, 0:SLOT, at] = lax.dot_general(
+            pick, rep_in[:, at], (((0,), (0,)), ((), ())), preferred_element_type=jnp.float32
+        ).astype(jnp.bfloat16)
+        xfull[my_y, SLOT : SLOT + 16, at] = jnp.broadcast_to(
+            gain_ref[:, at].astype(jnp.float32), (16, tile)
+        ).astype(jnp.bfloat16)
+        return carry
+
+    lax.fori_loop(0, tiles, unpack, 0)
+    across = remote(xfull.at[my_y], xfull.at[my_y], y_s, y_r, mp=1 - my_y)
+    across.start()
+    grad_start, grad_finish = swap(grad_out, grad_in, grad_s, grad_r)
+    grad_start()
+    grad_in[mine, :] = grad_out[mine, :]
+
+    hrows = wrows // 2
+    own_x.wait_recv()
+    x_on = send_w(3, flip(rel, 2), 4, 0, hrows)
+    x_on.start()
+    x_core = send_w(4, flip(rel, 2), 1)
+    x_core.start()
+    own_z.wait_recv()
+    z_on = send_w(5, flip(rel, 4), 2, hrows, hrows)
+    z_on.start()
+    z_core = send_w(6, flip(rel, 4), 1)
+    z_core.start()
+
+    across.wait_send()
+    across.wait_recv()
+
+    def squares(j, total):
+        at = column(j)
+        a = xfull[0, 0:SLOT, at].astype(jnp.float32)
+        b = xfull[1, 0:SLOT, at].astype(jnp.float32)
+        return total + jnp.sum(a * a, axis=1, keepdims=True) + jnp.sum(
+            b * b, axis=1, keepdims=True
+        )
+
+    square_sums = lax.fori_loop(0, tiles, squares, jnp.zeros((SLOT, 1), jnp.float32))
+    scale = lax.rsqrt(square_sums / D + 1e-06)
+
+    def normed_at(h, at):
+        return (
+            xfull[h, 0:SLOT, at].astype(jnp.float32)
+            * scale
+            * xfull[h, SLOT : SLOT + 1, at].astype(jnp.float32)
+        ).astype(jnp.bfloat16)
+
+    def norm_far(j, carry):
+        at = column(j)
+        xsend[:, at] = normed_at(1 - half, at)
+        return carry
+
+    def norm_near(j, carry):
+        at = column(j)
+        xown[:, at] = normed_at(half, at)
+        return carry
+
+    lax.fori_loop(0, tiles, norm_far, 0)
+    far = flip(me, 8)
+    rows_out = remote(xsend, xpart, x_s, x_r, dp=far)
+    rows_out.start()
+    lax.fori_loop(0, tiles, norm_near, 0)
+
+    x_on.wait_recv()
+    z_on.wait_recv()
+    diag_core = send_w(7, flip(flip(rel, 2), 4), 1)
+    diag_core.start()
+    own_c.wait_recv()
+    x_core.wait_recv()
+    z_core.wait_recv()
+    rows_out.wait_send()
+    rows_out.wait_recv()
+    diag_core.wait_recv()
+
+    wide = 256
+    sends = []
+    for k in range(3):
+
+        def project(j, carry, k=k):
+            at = pl.ds(pl.multiple_of(j * wide, wide), wide)
+            weights = wbuf[k, :, at]
+            both = jnp.dot(
+                jnp.concatenate([xpart[...], xown[...]], axis=0),
+                weights,
+                preferred_element_type=jnp.float32,
+            )
+            part_out[k, :, at] = both[:SLOT].astype(jnp.bfloat16)
+            part_own[k, :, at] = both[SLOT:]
+            return carry
+
+        lax.fori_loop(0, qw // wide, project, 0)
+        send = remote(part_out.at[k], part_in.at[k], p_s.at[k], p_r.at[k], dp=far)
+        send.start()
+        sends.append(send)
+
+    grad_finish()
+
+    def credit(j, carry):
+        at = column(j)
+        gsum_ref[:, at] = lax.dot_general(
+            want, grad_in[:, at], (((0,), (0,)), ((), ())), preferred_element_type=jnp.float32
+        )
+        return carry
+
+    lax.fori_loop(0, tiles, credit, 0)
+    for copy in (own_x, own_z, own_c, x_on, x_core, z_on, z_core, diag_core):
+        copy.wait_send()
+    for send in sends:
+        send.wait_send()
+        send.wait_recv()
+
+    length = small_ref[8:9, :]
+    key_at = lax.broadcasted_iota(jnp.int32, (SLOT, SLOT), 1)
+    query_at = lax.broadcasted_iota(jnp.int32, (SLOT, SLOT), 0)
+    allowed = (key_at <= query_at) & (key_at < length)
+    live = query_at < length
+
+    def head(h, carry):
+        at = pl.ds(pl.multiple_of(h * HD, HD), HD)
+        query, keys, values = [
+            (part_own[k, :, at] + part_in[k, :, at].astype(jnp.float32)).astype(jnp.bfloat16)
+            for k in range(3)
+        ]
+        scores = lax.dot_general(
+            query, keys, (((1,), (1,)), ((), ())), preferred_element_type=jnp.float32
+        ) / math.sqrt(HD)
+        scores = jnp.where(allowed, scores, jnp.float32(-1e30))
+        powers = jnp.exp(scores - jnp.max(scores, axis=-1, keepdims=True))
+        probs = (powers / jnp.sum(powers, axis=-1, keepdims=True)).astype(jnp.bfloat16)
+        context = jnp.dot(probs, values, preferred_element_type=jnp.float32)
+        ctx_ref[:, at] = jnp.where(live, context, jnp.float32(0.0)).astype(jnp.bfloat16)
+        return carry
+
+    lax.fori_loop(0, qw // HD, head, 0)
+
+
+def local_16(
+    session_length, event_owner, event_row, text_rows, image_rows, price, price_dir, norm_gain,
+    w_query, w_key, w_value, cotangent,
+):
+    n = 16
+    cap = 16
+    tokens = event_row.shape[0]
+    width = text_rows.shape[1]
+    table = text_rows.shape[0]
+    wrows, qw = w_query.shape
+    owner_ids = event_owner[:, 0]
+    order = jnp.arange(tokens, dtype=jnp.int32)
+    earlier = jnp.sum(
+        ((owner_ids[:, None] == owner_ids[None, :]) & (order[:, None] < order[None, :])).astype(
+            jnp.int32
+        ),
+        axis=0,
+    )
+    slot_ids = owner_ids * cap + earlier
+    pick = slot_ids[None, :] == jnp.arange(n * cap, dtype=jnp.int32)[:, None]
+    asked = jnp.max(jnp.where(pick, event_row[None, :], -1), axis=1)
+    reqs = jnp.broadcast_to(asked[:, None], (n * cap, 128))
+    small = jnp.concatenate(
+        [
+            jnp.broadcast_to(slot_ids[None, :], (8, tokens)),
+            jnp.broadcast_to(session_length[:, None], (8, tokens)),
+        ]
+    )
+    vmem = pl.BlockSpec(memory_space=pltpu.VMEM)
+    hbm = pl.BlockSpec(memory_space=pl.ANY)
+    dma = pltpu.SemaphoreType.DMA
+    bf16 = jnp.bfloat16
+    context, gsum = pl.pallas_call(
+        exchange_kernel,
+        out_shape=(
+            jax.ShapeDtypeStruct((tokens, qw), bf16),
+            jax.ShapeDtypeStruct((table, width), jnp.float32),
+        ),
+        in_specs=[vmem] * 8 + [hbm] * 3,
+        out_specs=(vmem, vmem),
+        scratch_shapes=[
+            pltpu.VMEM((n * cap, 128), jnp.int32),
+            pltpu.VMEM((n * cap, width), bf16),
+            pltpu.VMEM((n * cap, width), bf16),
+            pltpu.VMEM((n * cap, width), bf16),
+            pltpu.VMEM((n * cap, width), bf16),
+            pltpu.VMEM((3, 8 * wrows, qw), bf16),
+            pltpu.VMEM((2, tokens + 16, width), bf16),
+            pltpu.VMEM((tokens, width), bf16),
+            pltpu.VMEM((tokens, width), bf16),
+            pltpu.VMEM((tokens, width), bf16),
+            pltpu.VMEM((3, tokens, qw), jnp.float32),
+            pltpu.VMEM((3, tokens, qw), bf16),
+            pltpu.VMEM((3, tokens, qw), bf16),
+            dma((3,)), dma((n,)), dma((n,)), dma((n,)), dma((n,)), dma((n,)), dma((n,)),
+            dma((8,)), dma((8,)), dma, dma, dma, dma, dma((3,)), dma((3,)),
+        ],
+        compiler_params=pltpu.CompilerParams(
+            collective_id=0, has_side_effects=True, vmem_limit_bytes=48 * 1024 * 1024
+        ),
+    )(
+        reqs, small, price[:, None], price_dir[None, :], norm_gain[None, :],
+        text_rows, image_rows, cotangent, w_query, w_key, w_value,
+    )
+    text_grad = gsum * image_rows.astype(jnp.float32)
+    image_grad = gsum * text_rows.astype(jnp.float32)
+    return (context, text_grad, image_grad)
+
+
 def solution(mesh):
+    fits = mesh.shape["dp"] == 16 and mesh.shape["mp"] == 2
     return jax.shard_map(
-        local,
+        local_16 if fits else local_any,
         mesh=mesh,
         in_specs=(
             P("dp"),

time: 358 us -> 168 us (0.47)
  waiting for transfers between devices: 270 us -> 0 us
  Pallas kernels: 0 us -> 150 us
  starting transfers between devices: 18.1 us -> 0 us
  matrix products: 14.8 us -> 0 us
  other arithmetic: 20.6 us -> 6.58 us
  between operations: 14.6 us -> 1.33 us
  blocking collectives: 4.93 us -> 0 us
  local copies, waits for them, and re-layouts: 13.5 us -> 9.61 us
    all_gather x4 -> x0, waiting for transfers between devices: 226 us -> none  [the longest x1 77.1 us: local(): value_sum = add_rows(lax.all_gather(w_value, 'dp', axis=0, tiled=True))]
    pallas_call x0 -> x1, Pallas kernels: none -> 150 us  [local_16(): pl.pallas_call(exchange_kernel, out_shape=(jax.ShapeDtypeStruct((tokens,...]
    all_to_all x3 -> x0, waiting for transfers between devices: 42.3 us -> none  [the longest x1 22.9 us: answer(): lax.all_to_all(joined_rows, 'dp', split_axis=0, concat_axis=0, tiled=True)]
    all_to_all x3 -> x0, starting transfers between devices: 18 us -> none  [the longest x1 7.36 us: local(): lax.all_to_all(requests, 'dp', split_axis=0, concat_axis=0, tiled=True)]
    dot_general x5 -> x0, matrix products: 14.8 us -> none  [the longest x3 14.2 us: add_rows(): jnp.dot(features_all, weight_rows, preferred_element_type=jnp.float32)]
    scatter-add x2 -> x0, other arithmetic: 12.4 us -> none  [the longest x1 6.22 us: credit_rows(): jax.ops.segment_sum(image_terms, flat_ids, num_segments=table_rows)]
    gather x5 -> x0, local copies, waits for them, and re-layouts: 7.63 us -> none  [the longest x2 4.68 us: fetch_rows(): return (row_ids, text_rows[row_ids], image_rows[row_ids])]
    unnamed x15 -> x13, local copies, waits for them, and re-layouts: 0.89 us -> 7.31 us
  transfers between devices with their start and end apart: 7 -> 0, of which waited for: 7 -> 0; matrix products, arithmetic and copies ran while one was open for 9% -> 0% of each run, Pallas kernels for 0% -> 0%
where the time goes in v1:
time: 168 us; the launch traced here: 167 us
  Pallas kernels  150 us (89%)
  local copies, waits for them, and re-layouts  9.61 us (6%)
  other arithmetic  6.58 us (4%)
    pallas_call x1, Pallas kernels, local_16(): pl.pallas_call(exchange_kernel, out_shape=(jax.ShapeDtypeStruct((tokens,...  150 us
    unnamed x13, local copies, waits for them, and re-layouts  7.31 us
    mul x1, other arithmetic, local_16(): image_grad = gsum * text_rows.astype(jnp.float32)  4.32 us

profile of v1, /device:TPU:0, one launch (start us, length us, event | category | flops | bytes accessed | tf_op | source)
XLA Modules:
  0.0 167.4 jit_solution(2136740488737887977)
XLA Ops:
  1.3 0.8 convert_reduce_fusion
  2.1 0.7 multiply_add_fusion
  2.8 0.8 select_reduce_fusion
  3.6 0.7 broadcast_in_dim.50.dir_ref
  4.3 0.7 broadcast_in_dim.51.gain_ref
  4.9 0.1 broadcast_in_dim.26.reqs_ref
  5.0 0.8 copy.16.price_ref
  5.9 0.0 copy-start
  5.9 1.2 copy-done
  7.1 0.0 copy-start.1
  7.1 1.2 copy-done.1
  8.3 0.0 copy-start.2
  8.3 1.0 copy-done.2
  9.4 0.0 copy-start.3
  9.4 1.0 copy-done.3
  10.4 0.0 copy-start.4
  10.4 1.0 copy-done.4
  11.4 0.0 copy-start.5
  11.4 1.0 copy-done.5
  12.5 149.9 %shard_map.139 = (bf16[128,1024]{1,0:T(8,128)(2,1)S(1)}, f32[256,2048]{1,0:T(8,128)}) custom-call(s32[256,128]{1,0:T(8,128)S(1)} %broadcast_in_dim.26.reqs_ref, s32[16,128]{1,0:T(8,128)S(1)} %concatenate.3.small_ref, f32[256,1]{1,0:T(8,128)S(1)} %copy.16.price_ref, bf16[1,2048]{1,0:T(2,128)(2,1)S(1)} %broadcast_in_dim.50.dir_ref, ...), custom_call_target="tpu_custom_call" | custom-call | tf_op jit(solution)/shard_map/pallas_call | solution.py:445
  162.4 4.3 %convert_multiply_fusion = (f32[256,2048]{1,0:T(8,128)}, f32[256,2048]{1,0:T(8,128)}) fusion(f32[256,2048]{1,0:T(8,128)} %get-tuple-element.6, bf16[256,2048]{1,0:T(8,128)(2,1)S(1)} %copy-done, bf16[256,2048]{1,0:T(8,128)(2,1)S(1)} %copy-done.1), kind=kLoop, calls=%fused_computation | loop fusion | flops 2097152 | bytes 8388608 | tf_op jit(solution)/shard_map/mul | solution.py:478
  166.7 0.7 copy.19
  (2 shorter events, 0.0 us)
Async XLA Ops:
  5.9 1.2 copy-start
  7.1 1.2 copy-start.1
  8.3 1.0 copy-start.2
  9.4 1.0 copy-start.3
  10.4 1.0 copy-start.4
  11.4 1.0 copy-start.5

commit v2 on v1

--- a/solution.py
+++ b/solution.py
@@ -146,12 +146,12 @@
 
 
 def exchange_kernel(
-    reqs_ref, small_ref, price_ref, dir_ref, gain_ref, text_ref, image_ref, cot_ref,
+    reqs_ref, small_ref, price_ref, dir_ref, gain_ref, text_hbm, image_hbm, cot_hbm,
     wq_ref, wk_ref, wv_ref,
     ctx_ref, gsum_ref,
-    ids, rep_out, rep_in, grad_out, grad_in, wbuf, xfull, xpart, xown, xsend, part_own,
-    part_out, part_in,
-    load_sem, id_s, id_r, rep_s, rep_r, grad_s, grad_r, w_s, w_r, y_s, y_r, x_s, x_r, p_s, p_r,
+    text_ref, image_ref, cot_ref, ids, slots, tq, tsend, rep_out, rep_in, grad_out, grad_in,
+    wbuf, xfull, xin, ss_out, ss_in, part_own, part_out, part_in,
+    load_sem, id_s, id_r, rep_s, rep_r, grad_s, grad_r, w_s, w_r, one_s, one_r, p_s, p_r,
 ):
     me = lax.axis_index("dp")
     my_y = lax.axis_index("mp")
@@ -159,13 +159,24 @@
     cap = 16
     rel = me % 8
     half = me // 8
+    far = flip(me, 8)
     wrows = wq_ref.shape[0]
     qw = wq_ref.shape[1]
-    loads = [
+    quarter = dir_ref.shape[1] // 2
+    table = text_ref.shape[0]
+    both_rows = 2 * SLOT
+    weights_in = (wq_ref, wk_ref, wv_ref)
+    table_loads = [
+        pltpu.make_async_copy(a, b, load_sem.at[3 + k])
+        for k, (a, b) in enumerate(
+            ((text_hbm, text_ref), (image_hbm, image_ref), (cot_hbm, cot_ref))
+        )
+    ]
+    w_loads = [
         pltpu.make_async_copy(w, wbuf.at[k, pl.ds(rel * wrows, wrows), :], load_sem.at[k])
-        for k, w in enumerate((wq_ref, wk_ref, wv_ref))
+        for k, w in enumerate(weights_in)
     ]
-    for load in loads:
+    for load in table_loads[:2] + w_loads + table_loads[2:]:
         load.start()
     barrier = pltpu.get_barrier_semaphore()
 
@@ -179,7 +190,11 @@
     pl.semaphore_signal(
         barrier, inc=1, device_id={"mp": 1 - my_y}, device_id_type=pl.DeviceIdType.MESH
     )
-    pl.semaphore_wait(barrier, n)
+    pl.semaphore_signal(
+        barrier, inc=1, device_id={"dp": far, "mp": 1 - my_y},
+        device_id_type=pl.DeviceIdType.MESH,
+    )
+    pl.semaphore_wait(barrier, n + 1)
 
     def remote(src, dst, send, recv, **to):
         return pltpu.make_async_remote_copy(
@@ -187,13 +202,10 @@
             device_id_type=pl.DeviceIdType.MESH,
         )
 
-    def swap(src, dst, send, recv):
+    def swap(src_of, dst, send, recv):
         def one(i):
             peer = (me + i) % n
-            return remote(
-                src.at[pl.ds(peer * cap, cap), :], dst.at[pl.ds(me * cap, cap), :],
-                send.at[i], recv.at[i], dp=peer,
-            )
+            return remote(src_of(peer), dst, send.at[i], recv.at[i], dp=peer)
 
         def start(i, carry):
             one(i).start()
@@ -209,178 +221,228 @@
             lambda: lax.fori_loop(1, n, finish, 0),
         )
 
-    mine = pl.ds(me * cap, cap)
-    id_start, id_finish = swap(reqs_ref, ids, id_s, id_r)
+    def block(peer):
+        return pl.ds(peer * cap, cap)
+
+    id_start, id_finish = swap(
+        lambda p: reqs_ref.at[block(p), :], ids.at[block(me), :], id_s, id_r
+    )
     id_start()
-    ids[mine, :] = reqs_ref[mine, :]
-
-    def shard(rel_index, low=0, count=wrows):
-        return wbuf.at[:, pl.ds(rel_index * wrows + low, count), :]
-
-    def send_w(k, rel_index, bit, low=0, count=wrows):
-        block = shard(rel_index, low, count)
-        return remote(block, block, w_s.at[k], w_r.at[k], dp=flip(me, bit))
-
-    for load in loads:
-        load.wait()
-    own_x, own_z, own_c = send_w(0, rel, 2), send_w(1, rel, 4), send_w(2, rel, 1)
-    own_x.start()
-    own_z.start()
-    own_c.start()
-
-    slot = small_ref[0:1, :]
-    pick = (
-        lax.broadcasted_iota(jnp.int32, (n * cap, SLOT), 0) == slot
-    ).astype(jnp.float32).astype(jnp.bfloat16)
+    slots[half] = small_ref[0:8, :]
+    slot_out = remote(
+        small_ref.at[pl.ds(0, 8), :], slots.at[half], one_s.at[0], one_r.at[0], dp=far
+    )
+    slot_out.start()
+    ids[block(me), :] = reqs_ref[block(me), :]
+
+    def send_w(k, c, rel_index, bit, low=0, count=wrows):
+        part = wbuf.at[k, pl.ds(rel_index * wrows + low, count), :]
+        return remote(part, part, w_s.at[8 * k + c], w_r.at[8 * k + c], dp=flip(me, bit))
+
+    hrows = wrows // 2
+    own_x = [send_w(k, 0, rel, 2) for k in range(3)]
+    own_z = [send_w(k, 1, rel, 4) for k in range(3)]
+    own_c = [send_w(k, 2, rel, 1) for k in range(3)]
+    x_on = [send_w(k, 3, flip(rel, 2), 4, 0, hrows) for k in range(3)]
+    x_core = [send_w(k, 4, flip(rel, 2), 1) for k in range(3)]
+    z_on = [send_w(k, 5, flip(rel, 4), 2, hrows, hrows) for k in range(3)]
+    z_core = [send_w(k, 6, flip(rel, 4), 1) for k in range(3)]
+    diag_core = [send_w(k, 7, flip(flip(rel, 2), 4), 1) for k in range(3)]
+
+    def pass_on(k):
+        own_x[k].wait_recv()
+        x_on[k].start()
+        x_core[k].start()
+        own_z[k].wait_recv()
+        z_on[k].start()
+        z_core[k].start()
+
+    def pass_diag(k):
+        x_on[k].wait_recv()
+        z_on[k].wait_recv()
+        diag_core[k].start()
+
+    table_loads[0].wait()
+    table_loads[1].wait()
     tile = 512
-    tiles = text_ref.shape[1] // tile
+    tiles = quarter // tile
+    price = price_ref[...]
+
+    def join(start, j):
+        src = pl.ds(pl.multiple_of(start + j * tile, tile), tile)
+        mixed = text_ref[:, src].astype(jnp.float32) * image_ref[:, src].astype(
+            jnp.float32
+        ) + price * dir_ref[:, src].astype(jnp.float32)
+        gain = jnp.broadcast_to(gain_ref[:, src].astype(jnp.float32), (16, tile))
+        return mixed.astype(jnp.bfloat16), gain.astype(jnp.bfloat16)
 
     def column(j):
         return pl.ds(pl.multiple_of(j * tile, tile), tile)
 
-    def pack_grads(j, carry):
-        at = column(j)
-        grad_out[:, at] = jnp.dot(
-            pick, cot_ref[:, at], preferred_element_type=jnp.float32
-        ).astype(jnp.bfloat16)
+    def join_out(j, carry):
+        rows, gain = join((1 - my_y) * quarter, j)
+        tsend[0:table, column(j)] = rows
+        tsend[table : table + 16, column(j)] = gain
         return carry
 
-    lax.fori_loop(0, tiles, pack_grads, 0)
+    def join_own(j, carry):
+        rows, gain = join(my_y * quarter, j)
+        tq[my_y, 0:table, column(j)] = rows
+        tq[my_y, table : table + 16, column(j)] = gain
+        return carry
+
+    lax.fori_loop(0, tiles, join_out, 0)
+    table_out = remote(tsend, tq.at[my_y], one_s.at[1], one_r.at[1], mp=1 - my_y)
+    table_out.start()
+    for k in range(3):
+        w_loads[k].wait()
+        own_x[k].start()
+        own_z[k].start()
+        own_c[k].start()
+    lax.fori_loop(0, tiles, join_own, 0)
+
+    def pick_of(slot):
+        return (
+            lax.broadcasted_iota(jnp.int32, (n * cap, SLOT), 0) == slot
+        ).astype(jnp.float32).astype(jnp.bfloat16)
+
     id_finish()
     got = ids[...]
     lane = lax.broadcasted_iota(jnp.int32, got.shape, 1)
-    table = text_ref.shape[0]
     want = jnp.concatenate(
         [(got == lane + 128 * k).astype(jnp.float32) for k in range(table // 128)], axis=1
     ).astype(jnp.bfloat16)
-    price = price_ref[...]
-
-    def reply(j, carry):
-        at = column(j)
-        mixed = text_ref[:, at].astype(jnp.float32) * image_ref[:, at].astype(
-            jnp.float32
-        ) + price * dir_ref[:, at].astype(jnp.float32)
-        rep_out[:, at] = jnp.dot(
-            want, mixed.astype(jnp.bfloat16), preferred_element_type=jnp.float32
+    table_out.wait_send()
+    table_out.wait_recv()
+    for m in range(2):
+
+        def reply(j, carry, m=m):
+            rows = jnp.dot(
+                want, tq[m, 0:table, column(j)], preferred_element_type=jnp.float32
+            ).astype(jnp.bfloat16)
+            rep_out[m, 0, :, column(j)] = rows[: 8 * cap]
+            rep_out[m, 1, :, column(j)] = rows[8 * cap :]
+            return carry
+
+        lax.fori_loop(0, tiles, reply, 0)
+    rep_start, rep_finish = swap(
+        lambda p: rep_out.at[p // 8, :, block(p % 8), :], rep_in.at[:, block(me), :],
+        rep_s, rep_r,
+    )
+    rep_start()
+    rep_in[:, block(me), :] = rep_out[half, :, block(rel), :]
+    table_loads[2].wait()
+    pick = pick_of(small_ref[0:1, :])
+
+    def pack_grads(j, carry):
+        grad_out[:, column(j)] = jnp.dot(
+            pick, cot_ref[:, column(j)], preferred_element_type=jnp.float32
         ).astype(jnp.bfloat16)
         return carry
 
-    lax.fori_loop(0, tiles, reply, 0)
-    rep_start, rep_finish = swap(rep_out, rep_in, rep_s, rep_r)
-    rep_start()
-    rep_in[mine, :] = rep_out[mine, :]
+    lax.fori_loop(0, 2 * tiles, pack_grads, 0)
+    pass_on(0)
+    slot_out.wait_send()
+    slot_out.wait_recv()
     rep_finish()
 
-    def unpack(j, carry):
-        at = column(j)
-        xfull[my_y, 0:SLOT, at] = lax.dot_general(
-            pick, rep_in[:, at], (((0,), (0,)), ((), ())), preferred_element_type=jnp.float32
-        ).astype(jnp.bfloat16)
-        xfull[my_y, SLOT : SLOT + 16, at] = jnp.broadcast_to(
-            gain_ref[:, at].astype(jnp.float32), (16, tile)
-        ).astype(jnp.bfloat16)
-        return carry
-
-    lax.fori_loop(0, tiles, unpack, 0)
-    across = remote(xfull.at[my_y], xfull.at[my_y], y_s, y_r, mp=1 - my_y)
+    for zs in range(2):
+        chosen = pick_of(slots[zs, 0:1, :])
+
+        def unpack(j, carry, zs=zs, chosen=chosen):
+            xfull[my_y, zs * SLOT : (zs + 1) * SLOT, column(j)] = lax.dot_general(
+                chosen, rep_in[zs, :, column(j)], (((0,), (0,)), ((), ())),
+                preferred_element_type=jnp.float32,
+            ).astype(jnp.bfloat16)
+            return carry
+
+        lax.fori_loop(0, tiles, unpack, 0)
+    xfull[my_y, both_rows : both_rows + 16, :] = tq[half, table : table + 16, :]
+    across = remote(xfull.at[my_y], xfull.at[my_y], one_s.at[2], one_r.at[2], mp=1 - my_y)
     across.start()
-    grad_start, grad_finish = swap(grad_out, grad_in, grad_s, grad_r)
+
+    def squares(q):
+        def add(j, total):
+            a = xfull[q, 0:both_rows, column(j)].astype(jnp.float32)
+            return total + jnp.sum(a * a, axis=1, keepdims=True)
+
+        return lax.fori_loop(0, tiles, add, jnp.zeros((both_rows, 1), jnp.float32))
+
+    near = squares(my_y)
+    ss_out[...] = jnp.transpose(jnp.broadcast_to(near, (both_rows, 128)))[0:8, :]
+    ss_far = remote(ss_out, ss_in.at[0], one_s.at[3], one_r.at[3], dp=far)
+    ss_far.start()
+    ss_diag = remote(ss_out, ss_in.at[1], one_s.at[4], one_r.at[4], dp=far, mp=1 - my_y)
+    ss_diag.start()
+    pass_on(1)
+    pass_diag(0)
+    pass_on(2)
+    grad_start, grad_finish = swap(
+        lambda p: grad_out.at[block(p), :], grad_in.at[block(me), :], grad_s, grad_r
+    )
     grad_start()
-    grad_in[mine, :] = grad_out[mine, :]
-
-    hrows = wrows // 2
-    own_x.wait_recv()
-    x_on = send_w(3, flip(rel, 2), 4, 0, hrows)
-    x_on.start()
-    x_core = send_w(4, flip(rel, 2), 1)
-    x_core.start()
-    own_z.wait_recv()
-    z_on = send_w(5, flip(rel, 4), 2, hrows, hrows)
-    z_on.start()
-    z_core = send_w(6, flip(rel, 4), 1)
-    z_core.start()
-
+    grad_in[block(me), :] = grad_out[block(me), :]
     across.wait_send()
     across.wait_recv()
-
-    def squares(j, total):
-        at = column(j)
-        a = xfull[0, 0:SLOT, at].astype(jnp.float32)
-        b = xfull[1, 0:SLOT, at].astype(jnp.float32)
-        return total + jnp.sum(a * a, axis=1, keepdims=True) + jnp.sum(
-            b * b, axis=1, keepdims=True
-        )
-
-    square_sums = lax.fori_loop(0, tiles, squares, jnp.zeros((SLOT, 1), jnp.float32))
-    scale = lax.rsqrt(square_sums / D + 1e-06)
-
-    def normed_at(h, at):
-        return (
-            xfull[h, 0:SLOT, at].astype(jnp.float32)
-            * scale
-            * xfull[h, SLOT : SLOT + 1, at].astype(jnp.float32)
-        ).astype(jnp.bfloat16)
-
-    def norm_far(j, carry):
-        at = column(j)
-        xsend[:, at] = normed_at(1 - half, at)
-        return carry
-
-    def norm_near(j, carry):
-        at = column(j)
-        xown[:, at] = normed_at(half, at)
-        return carry
-
-    lax.fori_loop(0, tiles, norm_far, 0)
-    far = flip(me, 8)
-    rows_out = remote(xsend, xpart, x_s, x_r, dp=far)
-    rows_out.start()
-    lax.fori_loop(0, tiles, norm_near, 0)
-
-    x_on.wait_recv()
-    z_on.wait_recv()
-    diag_core = send_w(7, flip(flip(rel, 2), 4), 1)
-    diag_core.start()
-    own_c.wait_recv()
-    x_core.wait_recv()
-    z_core.wait_recv()
-    rows_out.wait_send()
-    rows_out.wait_recv()
-    diag_core.wait_recv()
+    near = near + squares(1 - my_y)
+    for copy in (ss_far, ss_diag):
+        copy.wait_send()
+        copy.wait_recv()
+    beyond = ss_in[0] + ss_in[1]
+    beyond = jnp.transpose(jnp.broadcast_to(beyond[0:1, :], (128, both_rows)))[:, 0:1]
+    scale = lax.rsqrt((near + beyond) / D + 1e-06)
+    for q in range(2):
+
+        def norm(j, carry, q=q):
+            normed = (
+                xfull[q, 0:both_rows, column(j)].astype(jnp.float32)
+                * scale
+                * xfull[q, both_rows : both_rows + 1, column(j)].astype(jnp.float32)
+            )
+            xin[:, column(q * tiles + j)] = normed.astype(jnp.bfloat16)
+            return carry
+
+        lax.fori_loop(0, tiles, norm, 0)
 
     wide = 256
     sends = []
     for k in range(3):
+        if k:
+            pass_diag(k)
+        own_c[k].wait_recv()
+        x_core[k].wait_recv()
+        z_core[k].wait_recv()
+        diag_core[k].wait_recv()
 
         def project(j, carry, k=k):
             at = pl.ds(pl.multiple_of(j * wide, wide), wide)
-            weights = wbuf[k, :, at]
-            both = jnp.dot(
-                jnp.concatenate([xpart[...], xown[...]], axis=0),
-                weights,
-                preferred_element_type=jnp.float32,
-            )
-            part_out[k, :, at] = both[:SLOT].astype(jnp.bfloat16)
-            part_own[k, :, at] = both[SLOT:]
+            both = jnp.dot(xin[...], wbuf[k, :, at], preferred_element_type=jnp.float32)
+            for zs in range(2):
+                rows = both[zs * SLOT : (zs + 1) * SLOT]
+                part_own[k, zs, :, at] = rows
+                part_out[k, zs, :, at] = rows.astype(jnp.bfloat16)
             return carry
 
         lax.fori_loop(0, qw // wide, project, 0)
-        send = remote(part_out.at[k], part_in.at[k], p_s.at[k], p_r.at[k], dp=far)
+        send = remote(
+            part_out.at[k, 1 - half], part_in.at[k], p_s.at[k], p_r.at[k], dp=far
+        )
         send.start()
         sends.append(send)
 
     grad_finish()
 
     def credit(j, carry):
-        at = column(j)
-        gsum_ref[:, at] = lax.dot_general(
-            want, grad_in[:, at], (((0,), (0,)), ((), ())), preferred_element_type=jnp.float32
+        gsum_ref[:, column(j)] = lax.dot_general(
+            want, grad_in[:, column(j)], (((0,), (0,)), ((), ())),
+            preferred_element_type=jnp.float32,
         )
         return carry
 
-    lax.fori_loop(0, tiles, credit, 0)
-    for copy in (own_x, own_z, own_c, x_on, x_core, z_on, z_core, diag_core):
-        copy.wait_send()
+    lax.fori_loop(0, 2 * tiles, credit, 0)
+    for group in (own_x, own_z, own_c, x_on, x_core, z_on, z_core, diag_core):
+        for copy in group:
+            copy.wait_send()
     for send in sends:
         send.wait_send()
         send.wait_recv()
@@ -394,7 +456,9 @@
     def head(h, carry):
         at = pl.ds(pl.multiple_of(h * HD, HD), HD)
         query, keys, values = [
-            (part_own[k, :, at] + part_in[k, :, at].astype(jnp.float32)).astype(jnp.bfloat16)
+            (part_own[k, half, :, at] + part_in[k, :, at].astype(jnp.float32)).astype(
+                jnp.bfloat16
+            )
             for k in range(3)
         ]
         scores = lax.dot_general(
@@ -448,27 +512,33 @@
             jax.ShapeDtypeStruct((tokens, qw), bf16),
             jax.ShapeDtypeStruct((table, width), jnp.float32),
         ),
-        in_specs=[vmem] * 8 + [hbm] * 3,
+        in_specs=[vmem] * 5 + [hbm] * 6,
         out_specs=(vmem, vmem),
         scratch_shapes=[
+            pltpu.VMEM((table, width), bf16),
+            pltpu.VMEM((table, width), bf16),
+            pltpu.VMEM((tokens, width), bf16),
             pltpu.VMEM((n * cap, 128), jnp.int32),
-            pltpu.VMEM((n * cap, width), bf16),
-            pltpu.VMEM((n * cap, width), bf16),
+            pltpu.VMEM((2, 8, tokens), jnp.int32),
+            pltpu.VMEM((2, table + 16, width // 2), bf16),
+            pltpu.VMEM((table + 16, width // 2), bf16),
+            pltpu.VMEM((2, 2, 8 * cap, width // 2), bf16),
+            pltpu.VMEM((2, n * cap, width // 2), bf16),
             pltpu.VMEM((n * cap, width), bf16),
             pltpu.VMEM((n * cap, width), bf16),
             pltpu.VMEM((3, 8 * wrows, qw), bf16),
-            pltpu.VMEM((2, tokens + 16, width), bf16),
-            pltpu.VMEM((tokens, width), bf16),
-            pltpu.VMEM((tokens, width), bf16),
-            pltpu.VMEM((tokens, width), bf16),
-            pltpu.VMEM((3, tokens, qw), jnp.float32),
+            pltpu.VMEM((2, 2 * tokens + 16, width // 2), bf16),
+            pltpu.VMEM((2 * tokens, width), bf16),
+            pltpu.VMEM((8, 2 * tokens), jnp.float32),
+            pltpu.VMEM((2, 8, 2 * tokens), jnp.float32),
+            pltpu.VMEM((3, 2, tokens, qw), jnp.float32),
+            pltpu.VMEM((3, 2, tokens, qw), bf16),
             pltpu.VMEM((3, tokens, qw), bf16),
-            pltpu.VMEM((3, tokens, qw), bf16),
-            dma((3,)), dma((n,)), dma((n,)), dma((n,)), dma((n,)), dma((n,)), dma((n,)),
-            dma((8,)), dma((8,)), dma, dma, dma, dma, dma((3,)), dma((3,)),
+            dma((6,)), dma((n,)), dma((n,)), dma((n,)), dma((n,)), dma((n,)), dma((n,)),
+            dma((24,)), dma((24,)), dma((5,)), dma((5,)), dma((3,)), dma((3,)),
         ],
         compiler_params=pltpu.CompilerParams(
-            collective_id=0, has_side_effects=True, vmem_limit_bytes=48 * 1024 * 1024
+            collective_id=0, has_side_effects=True, vmem_limit_bytes=60 * 1024 * 1024
         ),
     )(
         reqs, small, price[:, None], price_dir[None, :], norm_gain[None, :],

time: 168 us -> 145 us (0.86)
  Pallas kernels: 150 us -> 131 us
  local copies, waits for them, and re-layouts: 9.61 us -> 6.11 us
    pallas_call x1, Pallas kernels: 150 us -> 131 us  [local_16(): pl.pallas_call(exchange_kernel, out_shape=(jax.ShapeDtypeStruct((tokens,...]
    unnamed x13 -> x7, local copies, waits for them, and re-layouts: 7.31 us -> 0.71 us
where the time goes in v2:
time: 145 us
  Pallas kernels  131 us (90%)
  other arithmetic  6.61 us (5%)
  local copies, waits for them, and re-layouts  6.11 us (4%)
    pallas_call x1, Pallas kernels, local_16(): pl.pallas_call(exchange_kernel, out_shape=(jax.ShapeDtypeStruct((tokens,...  131 us
    mul x1, other arithmetic, local_16(): image_grad = gsum * text_rows.astype(jnp.float32)  4.36 us

profile of v2, /device:TPU:0, one launch (start us, length us, event | category | flops | bytes accessed | tf_op | source)
XLA Modules:
  0.0 144.6 jit_solution(11948254350397587485)
XLA Ops:
  1.3 0.8 convert_reduce_fusion
  2.1 0.7 multiply_add_fusion
  2.8 0.8 select_reduce_fusion
  3.5 0.6 concatenate.3.small_ref
  4.1 1.3 broadcast_in_dim.50.dir_ref
  5.4 1.3 broadcast_in_dim.51.gain_ref
  6.7 0.8 broadcast_in_dim.26.reqs_ref
  7.5 1.5 %copy.16.price_ref = f32[256,1]{1,0:T(8,128)} copy(f32[256,1]{0,1:T(1,128)} %bitcast.5) | data formatting | bytes 2048 | tf_op jit(solution)/shard_map/broadcast_in_dim | solution.py:544
  8.9 0.0 copy-start
  8.9 0.0 copy-start.1
  8.9 130.6 %shard_map.139 = (bf16[128,1024]{1,0:T(8,128)(2,1)}, f32[256,2048]{1,0:T(8,128)}) custom-call(s32[256,128]{1,0:T(8,128)} %broadcast_in_dim.26.reqs_ref, s32[16,128]{1,0:T(8,128)} %concatenate.3.small_ref, f32[256,1]{1,0:T(8,128)} %copy.16.price_ref, bf16[1,2048]{1,0:T(2,128)(2,1)} %broadcast_in_dim.50.dir_ref, bf16[1,2048]{1,0:T(2,128)(2,1)} %broadcast_in_dim.51.gain_ref, ...), custom_call_target="tpu_custom_call" | custom-call | tf_op jit(solution)/shard_map/pallas_call | solution.py:509
  139.5 0.0 copy-done
  139.5 0.0 copy-done.1
  139.5 0.0 copy-start.2
  139.5 4.4 %convert_multiply_fusion = (f32[256,2048]{1,0:T(8,128)}, f32[256,2048]{1,0:T(8,128)}) fusion(f32[256,2048]{1,0:T(8,128)} %get-tuple-element.6, bf16[256,2048]{1,0:T(8,128)(2,1)S(1)} %copy-done, bf16[256,2048]{1,0:T(8,128)(2,1)S(1)} %copy-done.1), kind=kLoop, calls=%fused_computation | loop fusion | flops 2097152 | bytes 8388608 | tf_op jit(solution)/shard_map/mul | solution.py:548
  143.9 0.0 copy-done.2
  143.9 0.7 copy.19
  (1 shorter events, 0.0 us)
Async XLA Ops:
  8.9 130.6 %copy-start = (bf16[256,2048]{1,0:T(8,128)(2,1)S(1)}, bf16[256,2048]{1,0:T(8,128)(2,1)}, u32[]{:S(2)}) copy-start(bf16[256,2048]{1,0:T(8,128)(2,1)} %text_hbm.1) | copy-start | bytes 3145732
  8.9 130.6 %copy-start.1 = (bf16[256,2048]{1,0:T(8,128)(2,1)S(1)}, bf16[256,2048]{1,0:T(8,128)(2,1)}, u32[]{:S(2)}) copy-start(bf16[256,2048]{1,0:T(8,128)(2,1)} %image_hbm.1) | copy-start | bytes 3145732
  139.5 4.4 %copy-start.2 = (bf16[128,1024]{1,0:T(8,128)(2,1)S(1)}, bf16[128,1024]{1,0:T(8,128)(2,1)}, u32[]{:S(2)}) copy-start(bf16[128,1024]{1,0:T(8,128)(2,1)} %get-tuple-element.12) | copy-start | bytes 786436

commit v3 on v2

--- a/solution.py
+++ b/solution.py
@@ -146,11 +146,11 @@
 
 
 def exchange_kernel(
-    reqs_ref, small_ref, price_ref, dir_ref, gain_ref, text_hbm, image_hbm, cot_hbm,
+    length_ref, owner_ref, row_ref, price_ref, dir_ref, gain_ref, text_hbm, image_hbm, cot_hbm,
     wq_ref, wk_ref, wv_ref,
     ctx_ref, gsum_ref,
-    text_ref, image_ref, cot_ref, ids, slots, tq, tsend, rep_out, rep_in, grad_out, grad_in,
-    wbuf, xfull, xin, ss_out, ss_in, part_own, part_out, part_in,
+    text_ref, image_ref, cot_ref, reqs_ref, probs_ref, ids, slots, tq, tsend, rep_out, rep_in, grad_out, grad_in,
+    fvals, wbuf, xfull, xin, ss_out, ss_in, part_own, part_out, part_in,
     load_sem, id_s, id_r, rep_s, rep_r, grad_s, grad_r, w_s, w_r, one_s, one_r, p_s, p_r,
 ):
     me = lax.axis_index("dp")
@@ -162,7 +162,7 @@
     far = flip(me, 8)
     wrows = wq_ref.shape[0]
     qw = wq_ref.shape[1]
-    quarter = dir_ref.shape[1] // 2
+    quarter = dir_ref.shape[0] // 2
     table = text_ref.shape[0]
     both_rows = 2 * SLOT
     weights_in = (wq_ref, wk_ref, wv_ref)
@@ -176,8 +176,21 @@
         pltpu.make_async_copy(w, wbuf.at[k, pl.ds(rel * wrows, wrows), :], load_sem.at[k])
         for k, w in enumerate(weights_in)
     ]
-    for load in table_loads[:2] + w_loads + table_loads[2:]:
+    for load in w_loads + table_loads:
         load.start()
+    def lanes(ref, rows):
+        return jnp.broadcast_to(ref[...].reshape(1, ref.shape[0]), (rows, ref.shape[0]))
+
+    owner_along = lanes(owner_ref, SLOT)
+    before = lax.broadcasted_iota(jnp.int32, (SLOT, SLOT), 0) < lax.broadcasted_iota(
+        jnp.int32, (SLOT, SLOT), 1
+    )
+    same = (jnp.transpose(owner_along) == owner_along) & before
+    slot = owner_along[0:1, :] * cap + jnp.sum(same.astype(jnp.int32), axis=0, keepdims=True)
+    picked = lax.broadcasted_iota(jnp.int32, (n * cap, SLOT), 0) == slot
+    asked = jnp.max(jnp.where(picked, lanes(row_ref, n * cap), -1), axis=1, keepdims=True)
+    reqs_ref[...] = jnp.broadcast_to(asked, (n * cap, 128))
+    slots[half] = jnp.broadcast_to(slot, (8, SLOT))
     barrier = pltpu.get_barrier_semaphore()
 
     def greet(i, carry):
@@ -228,10 +241,7 @@
         lambda p: reqs_ref.at[block(p), :], ids.at[block(me), :], id_s, id_r
     )
     id_start()
-    slots[half] = small_ref[0:8, :]
-    slot_out = remote(
-        small_ref.at[pl.ds(0, 8), :], slots.at[half], one_s.at[0], one_r.at[0], dp=far
-    )
+    slot_out = remote(slots.at[half], slots.at[half], one_s.at[0], one_r.at[0], dp=far)
     slot_out.start()
     ids[block(me), :] = reqs_ref[block(me), :]
 
@@ -239,13 +249,13 @@
         part = wbuf.at[k, pl.ds(rel_index * wrows + low, count), :]
         return remote(part, part, w_s.at[8 * k + c], w_r.at[8 * k + c], dp=flip(me, bit))
 
-    hrows = wrows // 2
+    zrows = wrows // 4
     own_x = [send_w(k, 0, rel, 2) for k in range(3)]
     own_z = [send_w(k, 1, rel, 4) for k in range(3)]
     own_c = [send_w(k, 2, rel, 1) for k in range(3)]
-    x_on = [send_w(k, 3, flip(rel, 2), 4, 0, hrows) for k in range(3)]
+    x_on = [send_w(k, 3, flip(rel, 2), 4, 0, zrows) for k in range(3)]
     x_core = [send_w(k, 4, flip(rel, 2), 1) for k in range(3)]
-    z_on = [send_w(k, 5, flip(rel, 4), 2, hrows, hrows) for k in range(3)]
+    z_on = [send_w(k, 5, flip(rel, 4), 2, zrows, wrows - zrows) for k in range(3)]
     z_core = [send_w(k, 6, flip(rel, 4), 1) for k in range(3)]
     diag_core = [send_w(k, 7, flip(flip(rel, 2), 4), 1) for k in range(3)]
 
@@ -262,43 +272,47 @@
         z_on[k].wait_recv()
         diag_core[k].start()
 
-    table_loads[0].wait()
-    table_loads[1].wait()
-    tile = 512
-    tiles = quarter // tile
-    price = price_ref[...]
-
-    def join(start, j):
-        src = pl.ds(pl.multiple_of(start + j * tile, tile), tile)
-        mixed = text_ref[:, src].astype(jnp.float32) * image_ref[:, src].astype(
-            jnp.float32
-        ) + price * dir_ref[:, src].astype(jnp.float32)
-        gain = jnp.broadcast_to(gain_ref[:, src].astype(jnp.float32), (16, tile))
-        return mixed.astype(jnp.bfloat16), gain.astype(jnp.bfloat16)
-
-    def column(j):
-        return pl.ds(pl.multiple_of(j * tile, tile), tile)
-
-    def join_out(j, carry):
-        rows, gain = join((1 - my_y) * quarter, j)
-        tsend[0:table, column(j)] = rows
-        tsend[table : table + 16, column(j)] = gain
-        return carry
-
-    def join_own(j, carry):
-        rows, gain = join(my_y * quarter, j)
-        tq[my_y, 0:table, column(j)] = rows
-        tq[my_y, table : table + 16, column(j)] = gain
-        return carry
-
-    lax.fori_loop(0, tiles, join_out, 0)
-    table_out = remote(tsend, tq.at[my_y], one_s.at[1], one_r.at[1], mp=1 - my_y)
-    table_out.start()
     for k in range(3):
         w_loads[k].wait()
         own_x[k].start()
         own_z[k].start()
         own_c[k].start()
+    table_loads[0].wait()
+    table_loads[1].wait()
+    tile = 512
+    tiles = quarter // tile
+    price = jnp.transpose(lanes(price_ref, 128))[:, 0:1]
+    dir_row = dir_ref[...].astype(jnp.float32).reshape(1, 2 * quarter)
+    gain_row = gain_ref[...].astype(jnp.float32).reshape(1, 2 * quarter)
+    fvals[0:1, :] = dir_row
+    fvals[8:9, :] = gain_row
+
+    def join(start, j):
+        src = pl.ds(pl.multiple_of(start + j * tile, tile), tile)
+        mixed = text_ref[:, src].astype(jnp.float32) * image_ref[:, src].astype(
+            jnp.float32
+        ) + price * fvals[0:1, src]
+        gain = jnp.broadcast_to(fvals[8:9, src], (16, tile))
+        return mixed.astype(jnp.bfloat16), gain.astype(jnp.bfloat16)
+
+    def column(j):
+        return pl.ds(pl.multiple_of(j * tile, tile), tile)
+
+    def join_out(j, carry):
+        rows, gain = join((1 - my_y) * quarter, j)
+        tsend[0:table, column(j)] = rows
+        tsend[table : table + 16, column(j)] = gain
+        return carry
+
+    def join_own(j, carry):
+        rows, gain = join(my_y * quarter, j)
+        tq[my_y, 0:table, column(j)] = rows
+        tq[my_y, table : table + 16, column(j)] = gain
+        return carry
+
+    lax.fori_loop(0, tiles, join_out, 0)
+    table_out = remote(tsend, tq.at[my_y], one_s.at[1], one_r.at[1], mp=1 - my_y)
+    table_out.start()
     lax.fori_loop(0, tiles, join_own, 0)
 
     def pick_of(slot):
@@ -332,7 +346,7 @@
     rep_start()
     rep_in[:, block(me), :] = rep_out[half, :, block(rel), :]
     table_loads[2].wait()
-    pick = pick_of(small_ref[0:1, :])
+    pick = pick_of(slots[half, 0:1, :])
 
     def pack_grads(j, carry):
         grad_out[:, column(j)] = jnp.dot(
@@ -443,35 +457,43 @@
     for group in (own_x, own_z, own_c, x_on, x_core, z_on, z_core, diag_core):
         for copy in group:
             copy.wait_send()
-    for send in sends:
-        send.wait_send()
-        send.wait_recv()
-
-    length = small_ref[8:9, :]
     key_at = lax.broadcasted_iota(jnp.int32, (SLOT, SLOT), 1)
     query_at = lax.broadcasted_iota(jnp.int32, (SLOT, SLOT), 0)
+    length = length_ref[0]
     allowed = (key_at <= query_at) & (key_at < length)
     live = query_at < length
 
-    def head(h, carry):
-        at = pl.ds(pl.multiple_of(h * HD, HD), HD)
-        query, keys, values = [
-            (part_own[k, half, :, at] + part_in[k, :, at].astype(jnp.float32)).astype(
-                jnp.bfloat16
-            )
-            for k in range(3)
-        ]
+    def whole(k, at):
+        total = part_own[k, half, :, at] + part_in[k, :, at].astype(jnp.float32)
+        return total.astype(jnp.bfloat16)
+
+    def head_columns(h):
+        return pl.ds(pl.multiple_of(h * HD, HD), HD)
+
+    def head_probs(h, carry):
+        at = head_columns(h)
         scores = lax.dot_general(
-            query, keys, (((1,), (1,)), ((), ())), preferred_element_type=jnp.float32
+            whole(0, at), whole(1, at), (((1,), (1,)), ((), ())),
+            preferred_element_type=jnp.float32,
         ) / math.sqrt(HD)
         scores = jnp.where(allowed, scores, jnp.float32(-1e30))
         powers = jnp.exp(scores - jnp.max(scores, axis=-1, keepdims=True))
-        probs = (powers / jnp.sum(powers, axis=-1, keepdims=True)).astype(jnp.bfloat16)
-        context = jnp.dot(probs, values, preferred_element_type=jnp.float32)
+        probs_ref[h] = (powers / jnp.sum(powers, axis=-1, keepdims=True)).astype(jnp.bfloat16)
+        return carry
+
+    def head_context(h, carry):
+        at = head_columns(h)
+        context = jnp.dot(probs_ref[h], whole(2, at), preferred_element_type=jnp.float32)
         ctx_ref[:, at] = jnp.where(live, context, jnp.float32(0.0)).astype(jnp.bfloat16)
         return carry
 
-    lax.fori_loop(0, qw // HD, head, 0)
+    sends[0].wait_recv()
+    sends[1].wait_recv()
+    lax.fori_loop(0, qw // HD, head_probs, 0)
+    sends[2].wait_recv()
+    lax.fori_loop(0, qw // HD, head_context, 0)
+    for send in sends:
+        send.wait_send()
 
 
 def local_16(
@@ -484,24 +506,6 @@
     width = text_rows.shape[1]
     table = text_rows.shape[0]
     wrows, qw = w_query.shape
-    owner_ids = event_owner[:, 0]
-    order = jnp.arange(tokens, dtype=jnp.int32)
-    earlier = jnp.sum(
-        ((owner_ids[:, None] == owner_ids[None, :]) & (order[:, None] < order[None, :])).astype(
-            jnp.int32
-        ),
-        axis=0,
-    )
-    slot_ids = owner_ids * cap + earlier
-    pick = slot_ids[None, :] == jnp.arange(n * cap, dtype=jnp.int32)[:, None]
-    asked = jnp.max(jnp.where(pick, event_row[None, :], -1), axis=1)
-    reqs = jnp.broadcast_to(asked[:, None], (n * cap, 128))
-    small = jnp.concatenate(
-        [
-            jnp.broadcast_to(slot_ids[None, :], (8, tokens)),
-            jnp.broadcast_to(session_length[:, None], (8, tokens)),
-        ]
-    )
     vmem = pl.BlockSpec(memory_space=pltpu.VMEM)
     hbm = pl.BlockSpec(memory_space=pl.ANY)
     dma = pltpu.SemaphoreType.DMA
@@ -512,12 +516,14 @@
             jax.ShapeDtypeStruct((tokens, qw), bf16),
             jax.ShapeDtypeStruct((table, width), jnp.float32),
         ),
-        in_specs=[vmem] * 5 + [hbm] * 6,
+        in_specs=[pl.BlockSpec(memory_space=pltpu.SMEM)] + [vmem] * 5 + [hbm] * 6,
         out_specs=(vmem, vmem),
         scratch_shapes=[
             pltpu.VMEM((table, width), bf16),
             pltpu.VMEM((table, width), bf16),
             pltpu.VMEM((tokens, width), bf16),
+            pltpu.VMEM((n * cap, 128), jnp.int32),
+            pltpu.VMEM((qw // HD, tokens, tokens), bf16),
             pltpu.VMEM((n * cap, 128), jnp.int32),
             pltpu.VMEM((2, 8, tokens), jnp.int32),
             pltpu.VMEM((2, table + 16, width // 2), bf16),
@@ -526,6 +532,7 @@
             pltpu.VMEM((2, n * cap, width // 2), bf16),
             pltpu.VMEM((n * cap, width), bf16),
             pltpu.VMEM((n * cap, width), bf16),
+            pltpu.VMEM((16, width), jnp.float32),
             pltpu.VMEM((3, 8 * wrows, qw), bf16),
             pltpu.VMEM((2, 2 * tokens + 16, width // 2), bf16),
             pltpu.VMEM((2 * tokens, width), bf16),
@@ -541,7 +548,7 @@
             collective_id=0, has_side_effects=True, vmem_limit_bytes=60 * 1024 * 1024
         ),
     )(
-        reqs, small, price[:, None], price_dir[None, :], norm_gain[None, :],
+        session_length, event_owner[:, 0], event_row, price, price_dir, norm_gain,
         text_rows, image_rows, cotangent, w_query, w_key, w_value,
     )
     text_grad = gsum * image_rows.astype(jnp.float32)

time: 145 us -> 132 us (0.910)
  local copies, waits for them, and re-layouts: 6.11 us -> 0.72 us
  Pallas kernels: 131 us -> 126 us
  other arithmetic: 6.61 us -> 4.36 us
    broadcast_in_dim x5 -> x0, local copies, waits for them, and re-layouts: 4.79 us -> none  [the longest x1 1.47 us: local_16(): price[:, None]]
    pallas_call x1, Pallas kernels: 131 us -> 126 us  [local_16(): pl.pallas_call(exchange_kernel, out_shape=(jax.ShapeDtypeStruct((tokens,...]
where the time goes in v3:
time: 132 us
  Pallas kernels  126 us (95%)
  other arithmetic  4.36 us (3%)
  between operations  1.33 us (1%)
    pallas_call x1, Pallas kernels, local_16(): pl.pallas_call(exchange_kernel, out_shape=(jax.ShapeDtypeStruct((tokens,...  126 us
    mul x1, other arithmetic, local_16(): image_grad = gsum * text_rows.astype(jnp.float32)  4.36 us

profile of v3, /device:TPU:0, one launch (start us, length us, event | category | flops | bytes accessed | tf_op | source)
XLA Modules:
  0.0 132.3 jit_solution(1121079040801821103)
XLA Ops:
  1.3 0.0 copy-start
  1.3 0.0 copy-start.1
  1.3 125.9 %shard_map.139 = (bf16[128,1024]{1,0:T(8,128)(2,1)}, f32[256,2048]{1,0:T(8,128)}) custom-call(s32[1]{0:T(128)S(6)} %copy.16.length_ref, s32[128]{0:T(128)} %bitcast.1, s32[128]{0:T(128)} %row_ref.1, f32[256]{0:T(256)} %price_ref.1, bf16[2048]{0:T(1024)(128)(2,1)} %dir_ref.1, bf16[2048]{0:T(1024)(128)(2,1)} %gain_ref.1, bf16[256,2048]{1,0:T(8,128)(2,1)} %text_hbm.1, ...), custom_call_target="tpu_custom_call" | custom-call | tf_op jit(solution)/shard_map/pallas_call | solution.py:513
  127.2 0.0 copy-done
  127.2 0.0 copy-done.1
  127.2 0.0 copy-start.2
  127.2 4.4 %convert_multiply_fusion = (f32[256,2048]{1,0:T(8,128)}, f32[256,2048]{1,0:T(8,128)}) fusion(f32[256,2048]{1,0:T(8,128)} %get-tuple-element.6, bf16[256,2048]{1,0:T(8,128)(2,1)S(1)} %copy-done, bf16[256,2048]{1,0:T(8,128)(2,1)S(1)} %copy-done.1), kind=kLoop, calls=%fused_computation | loop fusion | flops 2097152 | bytes 8388608 | tf_op jit(solution)/shard_map/mul | solution.py:555
  131.6 0.0 copy-done.2
  131.6 0.7 copy.17
Async XLA Ops:
  1.3 125.9 %copy-start = (bf16[256,2048]{1,0:T(8,128)(2,1)S(1)}, bf16[256,2048]{1,0:T(8,128)(2,1)}, u32[]{:S(2)}) copy-start(bf16[256,2048]{1,0:T(8,128)(2,1)} %text_hbm.1) | copy-start | bytes 3145732
  1.3 125.9 %copy-start.1 = (bf16[256,2048]{1,0:T(8,128)(2,1)S(1)}, bf16[256,2048]{1,0:T(8,128)(2,1)}, u32[]{:S(2)}) copy-start(bf16[256,2048]{1,0:T(8,128)(2,1)} %image_hbm.1) | copy-start | bytes 3145732
  127.2 4.4 %copy-start.2 = (bf16[128,1024]{1,0:T(8,128)(2,1)S(1)}, bf16[128,1024]{1,0:T(8,128)(2,1)}, u32[]{:S(2)}) copy-start(bf16[128,1024]{1,0:T(8,128)(2,1)} %get-tuple-element.12) | copy-start | bytes 786436

commit v4 on v3

--- a/solution.py
+++ b/solution.py
@@ -178,6 +178,23 @@
     ]
     for load in w_loads + table_loads:
         load.start()
+    barrier = pltpu.get_barrier_semaphore()
+
+    def greet(i, carry):
+        pl.semaphore_signal(
+            barrier, inc=1, device_id={"dp": (me + i) % n}, device_id_type=pl.DeviceIdType.MESH
+        )
+        return carry
+
+    lax.fori_loop(1, n, greet, 0)
+    pl.semaphore_signal(
+        barrier, inc=1, device_id={"mp": 1 - my_y}, device_id_type=pl.DeviceIdType.MESH
+    )
+    pl.semaphore_signal(
+        barrier, inc=1, device_id={"dp": far, "mp": 1 - my_y},
+        device_id_type=pl.DeviceIdType.MESH,
+    )
+
     def lanes(ref, rows):
         return jnp.broadcast_to(ref[...].reshape(1, ref.shape[0]), (rows, ref.shape[0]))
 
@@ -191,22 +208,6 @@
     asked = jnp.max(jnp.where(picked, lanes(row_ref, n * cap), -1), axis=1, keepdims=True)
     reqs_ref[...] = jnp.broadcast_to(asked, (n * cap, 128))
     slots[half] = jnp.broadcast_to(slot, (8, SLOT))
-    barrier = pltpu.get_barrier_semaphore()
-
-    def greet(i, carry):
-        pl.semaphore_signal(
-            barrier, inc=1, device_id={"dp": (me + i) % n}, device_id_type=pl.DeviceIdType.MESH
-        )
-        return carry
-
-    lax.fori_loop(1, n, greet, 0)
-    pl.semaphore_signal(
-        barrier, inc=1, device_id={"mp": 1 - my_y}, device_id_type=pl.DeviceIdType.MESH
-    )
-    pl.semaphore_signal(
-        barrier, inc=1, device_id={"dp": far, "mp": 1 - my_y},
-        device_id_type=pl.DeviceIdType.MESH,
-    )
     pl.semaphore_wait(barrier, n + 1)
 
     def remote(src, dst, send, recv, **to):
@@ -272,10 +273,12 @@
         z_on[k].wait_recv()
         diag_core[k].start()
 
-    for k in range(3):
+    w_loads[0].wait()
+    own_x[0].start()
+    own_z[0].start()
+    own_c[0].start()
+    for k in (1, 2):
         w_loads[k].wait()
-        own_x[k].start()
-        own_z[k].start()
         own_c[k].start()
     table_loads[0].wait()
     table_loads[1].wait()
@@ -344,6 +347,7 @@
         rep_s, rep_r,
     )
     rep_start()
+    own_x[1].start()
     rep_in[:, block(me), :] = rep_out[half, :, block(rel), :]
     table_loads[2].wait()
     pick = pick_of(slots[half, 0:1, :])
@@ -359,6 +363,8 @@
     slot_out.wait_send()
     slot_out.wait_recv()
     rep_finish()
+    own_z[1].start()
+    own_x[2].start()
 
     for zs in range(2):
         chosen = pick_of(slots[zs, 0:1, :])
@@ -388,16 +394,13 @@
     ss_far.start()
     ss_diag = remote(ss_out, ss_in.at[1], one_s.at[4], one_r.at[4], dp=far, mp=1 - my_y)
     ss_diag.start()
-    pass_on(1)
     pass_diag(0)
-    pass_on(2)
     grad_start, grad_finish = swap(
         lambda p: grad_out.at[block(p), :], grad_in.at[block(me), :], grad_s, grad_r
     )
-    grad_start()
-    grad_in[block(me), :] = grad_out[block(me), :]
     across.wait_send()
     across.wait_recv()
+    own_z[2].start()
     near = near + squares(1 - my_y)
     for copy in (ss_far, ss_diag):
         copy.wait_send()
@@ -422,6 +425,10 @@
     sends = []
     for k in range(3):
         if k:
+            pass_on(k)
+            if k == 1:
+                grad_start()
+                grad_in[block(me), :] = grad_out[block(me), :]
             pass_diag(k)
         own_c[k].wait_recv()
         x_core[k].wait_recv()

time: 132 us -> 131 us (level)
  Pallas kernels: 126 us -> 124 us
    pallas_call x1, Pallas kernels: 126 us -> 124 us  [local_16(): pl.pallas_call(exchange_kernel, out_shape=(jax.ShapeDtypeStruct((tokens,...]
where the time goes in v4:
time: 131 us; the launch traced here: 130 us
  Pallas kernels  124 us (95%)
  other arithmetic  4.36 us (3%)
  between operations  1.33 us (1%)
    pallas_call x1, Pallas kernels, local_16(): pl.pallas_call(exchange_kernel, out_shape=(jax.ShapeDtypeStruct((tokens,...  124 us
    mul x1, other arithmetic, local_16(): image_grad = gsum * text_rows.astype(jnp.float32)  4.36 us

profile of v4, /device:TPU:0, one launch (start us, length us, event | category | flops | bytes accessed | tf_op | source)
XLA Modules:
  0.0 130.0 jit_solution(10000379071477709363)
XLA Ops:
  1.3 0.0 copy-start
  1.3 0.0 copy-start.1
  1.3 123.6 %shard_map.139 = (bf16[128,1024]{1,0:T(8,128)(2,1)}, f32[256,2048]{1,0:T(8,128)}) custom-call(s32[1]{0:T(128)S(6)} %copy.16.length_ref, s32[128]{0:T(128)} %bitcast.1, s32[128]{0:T(128)} %row_ref.1, f32[256]{0:T(256)} %price_ref.1, bf16[2048]{0:T(1024)(128)(2,1)} %dir_ref.1, bf16[2048]{0:T(1024)(128)(2,1)} %gain_ref.1, bf16[256,2048]{1,0:T(8,128)(2,1)} %text_hbm.1, ...), custom_call_target="tpu_custom_call" | custom-call | tf_op jit(solution)/shard_map/pallas_call | solution.py:520
  124.9 0.0 copy-done
  124.9 0.0 copy-done.1
  124.9 0.0 copy-start.2
  125.0 4.4 %convert_multiply_fusion = (f32[256,2048]{1,0:T(8,128)}, f32[256,2048]{1,0:T(8,128)}) fusion(f32[256,2048]{1,0:T(8,128)} %get-tuple-element.6, bf16[256,2048]{1,0:T(8,128)(2,1)S(1)} %copy-done, bf16[256,2048]{1,0:T(8,128)(2,1)S(1)} %copy-done.1), kind=kLoop, calls=%fused_computation | loop fusion | flops 2097152 | bytes 8388608 | tf_op jit(solution)/shard_map/mul | solution.py:562
  129.3 0.0 copy-done.2
  129.3 0.7 copy.17
Async XLA Ops:
  1.3 123.6 %copy-start = (bf16[256,2048]{1,0:T(8,128)(2,1)S(1)}, bf16[256,2048]{1,0:T(8,128)(2,1)}, u32[]{:S(2)}) copy-start(bf16[256,2048]{1,0:T(8,128)(2,1)} %text_hbm.1) | copy-start | bytes 3145732
  1.3 123.6 %copy-start.1 = (bf16[256,2048]{1,0:T(8,128)(2,1)S(1)}, bf16[256,2048]{1,0:T(8,128)(2,1)}, u32[]{:S(2)}) copy-start(bf16[256,2048]{1,0:T(8,128)(2,1)} %image_hbm.1) | copy-start | bytes 3145732
  124.9 4.4 %copy-start.2 = (bf16[128,1024]{1,0:T(8,128)(2,1)S(1)}, bf16[128,1024]{1,0:T(8,128)(2,1)}, u32[]{:S(2)}) copy-start(bf16[128,1024]{1,0:T(8,128)(2,1)} %get-tuple-element.12) | copy-start | bytes 786436

commit v5 on v4

--- a/solution.py
+++ b/solution.py
@@ -216,10 +216,10 @@
             device_id_type=pl.DeviceIdType.MESH,
         )
 
-    def swap(src_of, dst, send, recv):
+    def swap(src_of, dst, send, recv, base=0):
         def one(i):
             peer = (me + i) % n
-            return remote(src_of(peer), dst, send.at[i], recv.at[i], dp=peer)
+            return remote(src_of(peer), dst, send.at[base + i], recv.at[base + i], dp=peer)
 
         def start(i, carry):
             one(i).start()
@@ -313,9 +313,19 @@
         tq[my_y, table : table + 16, column(j)] = gain
         return carry
 
-    lax.fori_loop(0, tiles, join_out, 0)
-    table_out = remote(tsend, tq.at[my_y], one_s.at[1], one_r.at[1], mp=1 - my_y)
-    table_out.start()
+    def piece(c):
+        return pl.ds(c * tile, tile)
+
+    table_out = [
+        remote(
+            tsend.at[:, piece(c)], tq.at[my_y, :, piece(c)], one_s.at[5 + c], one_r.at[5 + c],
+            mp=1 - my_y,
+        )
+        for c in range(tiles)
+    ]
+    for c in range(tiles):
+        join_out(c, 0)
+        table_out[c].start()
     lax.fori_loop(0, tiles, join_own, 0)
 
     def pick_of(slot):
@@ -329,24 +339,24 @@
     want = jnp.concatenate(
         [(got == lane + 128 * k).astype(jnp.float32) for k in range(table // 128)], axis=1
     ).astype(jnp.bfloat16)
-    table_out.wait_send()
-    table_out.wait_recv()
-    for m in range(2):
-
-        def reply(j, carry, m=m):
+    replies = [
+        swap(
+            lambda p, c=c: rep_out.at[p // 8, :, block(p % 8), piece(c)],
+            rep_in.at[:, block(me), piece(c)],
+            rep_s, rep_r, c * n,
+        )
+        for c in range(tiles)
+    ]
+    for c in range(tiles):
+        table_out[c].wait_send()
+        table_out[c].wait_recv()
+        for m in range(2):
             rows = jnp.dot(
-                want, tq[m, 0:table, column(j)], preferred_element_type=jnp.float32
+                want, tq[m, 0:table, piece(c)], preferred_element_type=jnp.float32
             ).astype(jnp.bfloat16)
-            rep_out[m, 0, :, column(j)] = rows[: 8 * cap]
-            rep_out[m, 1, :, column(j)] = rows[8 * cap :]
-            return carry
-
-        lax.fori_loop(0, tiles, reply, 0)
-    rep_start, rep_finish = swap(
-        lambda p: rep_out.at[p // 8, :, block(p % 8), :], rep_in.at[:, block(me), :],
-        rep_s, rep_r,
-    )
-    rep_start()
+            rep_out[m, 0, :, piece(c)] = rows[: 8 * cap]
+            rep_out[m, 1, :, piece(c)] = rows[8 * cap :]
+        replies[c][0]()
     own_x[1].start()
     rep_in[:, block(me), :] = rep_out[half, :, block(rel), :]
     table_loads[2].wait()
@@ -362,24 +372,30 @@
     pass_on(0)
     slot_out.wait_send()
     slot_out.wait_recv()
-    rep_finish()
-    own_z[1].start()
-    own_x[2].start()
-
-    for zs in range(2):
-        chosen = pick_of(slots[zs, 0:1, :])
-
-        def unpack(j, carry, zs=zs, chosen=chosen):
-            xfull[my_y, zs * SLOT : (zs + 1) * SLOT, column(j)] = lax.dot_general(
-                chosen, rep_in[zs, :, column(j)], (((0,), (0,)), ((), ())),
+    chosen = [pick_of(slots[zs, 0:1, :]) for zs in range(2)]
+    across = []
+    for c in range(tiles):
+        replies[c][1]()
+        if c == tiles - 1:
+            own_z[1].start()
+            own_x[2].start()
+        for zs in range(2):
+            xfull[my_y, zs * SLOT : (zs + 1) * SLOT, piece(c)] = lax.dot_general(
+                chosen[zs], rep_in[zs, :, piece(c)], (((0,), (0,)), ((), ())),
                 preferred_element_type=jnp.float32,
             ).astype(jnp.bfloat16)
-            return carry
-
-        lax.fori_loop(0, tiles, unpack, 0)
-    xfull[my_y, both_rows : both_rows + 16, :] = tq[half, table : table + 16, :]
-    across = remote(xfull.at[my_y], xfull.at[my_y], one_s.at[2], one_r.at[2], mp=1 - my_y)
-    across.start()
+        xfull[my_y, both_rows : both_rows + 16, piece(c)] = tq[
+            half, table : table + 16, piece(c)
+        ]
+        part = xfull.at[my_y, :, piece(c)]
+        across.append(remote(part, part, one_s.at[1 + c], one_r.at[1 + c], mp=1 - my_y))
+        across[c].start()
+    grad_start, grad_finish = swap(
+        lambda p: grad_out.at[block(p), :], grad_in.at[block(me), :], grad_s, grad_r
+    )
+    grad_start()
+    own_z[2].start()
+    grad_in[block(me), :] = grad_out[block(me), :]
 
     def squares(q):
         def add(j, total):
@@ -395,12 +411,9 @@
     ss_diag = remote(ss_out, ss_in.at[1], one_s.at[4], one_r.at[4], dp=far, mp=1 - my_y)
     ss_diag.start()
     pass_diag(0)
-    grad_start, grad_finish = swap(
-        lambda p: grad_out.at[block(p), :], grad_in.at[block(me), :], grad_s, grad_r
-    )
-    across.wait_send()
-    across.wait_recv()
-    own_z[2].start()
+    for copy in across:
+        copy.wait_send()
+        copy.wait_recv()
     near = near + squares(1 - my_y)
     for copy in (ss_far, ss_diag):
         copy.wait_send()
@@ -426,9 +439,6 @@
     for k in range(3):
         if k:
             pass_on(k)
-            if k == 1:
-                grad_start()
-                grad_in[block(me), :] = grad_out[block(me), :]
             pass_diag(k)
         own_c[k].wait_recv()
         x_core[k].wait_recv()
@@ -444,26 +454,17 @@
                 part_out[k, zs, :, at] = rows.astype(jnp.bfloat16)
             return carry
 
-        lax.fori_loop(0, qw // wide, project, 0)
-        send = remote(
-            part_out.at[k, 1 - half], part_in.at[k], p_s.at[k], p_r.at[k], dp=far
-        )
-        send.start()
-        sends.append(send)
-
-    grad_finish()
-
-    def credit(j, carry):
-        gsum_ref[:, column(j)] = lax.dot_general(
-            want, grad_in[:, column(j)], (((0,), (0,)), ((), ())),
-            preferred_element_type=jnp.float32,
-        )
-        return carry
-
-    lax.fori_loop(0, 2 * tiles, credit, 0)
-    for group in (own_x, own_z, own_c, x_on, x_core, z_on, z_core, diag_core):
-        for copy in group:
-            copy.wait_send()
+        steps = qw // wide // 2
+        for h in range(2):
+            lax.fori_loop(h * steps, (h + 1) * steps, project, 0)
+            cols = pl.ds(h * (qw // 2), qw // 2)
+            send = remote(
+                part_out.at[k, 1 - half, :, cols], part_in.at[k, :, cols],
+                p_s.at[2 * k + h], p_r.at[2 * k + h], dp=far,
+            )
+            send.start()
+            sends.append(send)
+
     key_at = lax.broadcasted_iota(jnp.int32, (SLOT, SLOT), 1)
     query_at = lax.broadcasted_iota(jnp.int32, (SLOT, SLOT), 0)
     length = length_ref[0]
@@ -494,11 +495,26 @@
         ctx_ref[:, at] = jnp.where(live, context, jnp.float32(0.0)).astype(jnp.bfloat16)
         return carry
 
-    sends[0].wait_recv()
-    sends[1].wait_recv()
+    for send in sends[:4]:
+        send.wait_recv()
     lax.fori_loop(0, qw // HD, head_probs, 0)
-    sends[2].wait_recv()
-    lax.fori_loop(0, qw // HD, head_context, 0)
+    grad_finish()
+
+    def credit(j, carry):
+        gsum_ref[:, column(j)] = lax.dot_general(
+            want, grad_in[:, column(j)], (((0,), (0,)), ((), ())),
+            preferred_element_type=jnp.float32,
+        )
+        return carry
+
+    lax.fori_loop(0, 2 * tiles, credit, 0)
+    for group in (own_x, own_z, own_c, x_on, x_core, z_on, z_core, diag_core):
+        for copy in group:
+            copy.wait_send()
+    half_heads = qw // HD // 2
+    for h in range(2):
+        sends[4 + h].wait_recv()
+        lax.fori_loop(h * half_heads, (h + 1) * half_heads, head_context, 0)
     for send in sends:
         send.wait_send()
 
@@ -548,8 +564,8 @@
             pltpu.VMEM((3, 2, tokens, qw), jnp.float32),
             pltpu.VMEM((3, 2, tokens, qw), bf16),
             pltpu.VMEM((3, tokens, qw), bf16),
-            dma((6,)), dma((n,)), dma((n,)), dma((n,)), dma((n,)), dma((n,)), dma((n,)),
-            dma((24,)), dma((24,)), dma((5,)), dma((5,)), dma((3,)), dma((3,)),
+            dma((6,)), dma((n,)), dma((n,)), dma((2 * n,)), dma((2 * n,)), dma((n,)), dma((n,)),
+            dma((24,)), dma((24,)), dma((7,)), dma((7,)), dma((6,)), dma((6,)),
         ],
         compiler_params=pltpu.CompilerParams(
             collective_id=0, has_side_effects=True, vmem_limit_bytes=60 * 1024 * 1024

time: 131 us -> 133 us (1.015)
  Pallas kernels: 124 us -> 126 us
    pallas_call x1, Pallas kernels: 124 us -> 126 us  [local_16(): pl.pallas_call(exchange_kernel, out_shape=(jax.ShapeDtypeStruct((tokens,...]
where the time goes in v5:
time: 133 us
  Pallas kernels  126 us (95%)
  other arithmetic  4.36 us (3%)
  between operations  1.33 us (1%)
    pallas_call x1, Pallas kernels, local_16(): pl.pallas_call(exchange_kernel, out_shape=(jax.ShapeDtypeStruct((tokens,...  126 us
    mul x1, other arithmetic, local_16(): image_grad = gsum * text_rows.astype(jnp.float32)  4.36 us

profile of v5, /device:TPU:0, one launch (start us, length us, event | category | flops | bytes accessed | tf_op | source)
XLA Modules:
  0.0 132.5 jit_solution(8600220336864509343)
XLA Ops:
  1.3 0.0 copy-start
  1.3 0.0 copy-start.1
  1.3 126.1 %shard_map.139 = (bf16[128,1024]{1,0:T(8,128)(2,1)}, f32[256,2048]{1,0:T(8,128)}) custom-call(s32[1]{0:T(128)S(6)} %copy.16.length_ref, s32[128]{0:T(128)} %bitcast.1, s32[128]{0:T(128)} %row_ref.1, f32[256]{0:T(256)} %price_ref.1, bf16[2048]{0:T(1024)(128)(2,1)} %dir_ref.1, bf16[2048]{0:T(1024)(128)(2,1)} %gain_ref.1, bf16[256,2048]{1,0:T(8,128)(2,1)} %text_hbm.1, ...), custom_call_target="tpu_custom_call" | custom-call | tf_op jit(solution)/shard_map/pallas_call | solution.py:536
  127.4 0.0 copy-done
  127.5 0.0 copy-done.1
  127.5 0.0 copy-start.2
  127.5 4.4 %convert_multiply_fusion = (f32[256,2048]{1,0:T(8,128)}, f32[256,2048]{1,0:T(8,128)}) fusion(f32[256,2048]{1,0:T(8,128)} %get-tuple-element.6, bf16[256,2048]{1,0:T(8,128)(2,1)S(1)} %copy-done, bf16[256,2048]{1,0:T(8,128)(2,1)S(1)} %copy-done.1), kind=kLoop, calls=%fused_computation | loop fusion | flops 2097152 | bytes 8388608 | tf_op jit(solution)/shard_map/mul | solution.py:578
  131.8 0.0 copy-done.2
  131.8 0.7 copy.17
Async XLA Ops:
  1.3 126.2 %copy-start = (bf16[256,2048]{1,0:T(8,128)(2,1)S(1)}, bf16[256,2048]{1,0:T(8,128)(2,1)}, u32[]{:S(2)}) copy-start(bf16[256,2048]{1,0:T(8,128)(2,1)} %text_hbm.1) | copy-start | bytes 3145732
  1.3 126.2 %copy-start.1 = (bf16[256,2048]{1,0:T(8,128)(2,1)S(1)}, bf16[256,2048]{1,0:T(8,128)(2,1)}, u32[]{:S(2)}) copy-start(bf16[256,2048]{1,0:T(8,128)(2,1)} %image_hbm.1) | copy-start | bytes 3145732
  127.5 4.4 %copy-start.2 = (bf16[128,1024]{1,0:T(8,128)(2,1)S(1)}, bf16[128,1024]{1,0:T(8,128)(2,1)}, u32[]{:S(2)}) copy-start(bf16[128,1024]{1,0:T(8,128)(2,1)} %get-tuple-element.12) | copy-start | bytes 786436

commit v6 on v5

--- a/solution.py
+++ b/solution.py
@@ -250,7 +250,7 @@
         part = wbuf.at[k, pl.ds(rel_index * wrows + low, count), :]
         return remote(part, part, w_s.at[8 * k + c], w_r.at[8 * k + c], dp=flip(me, bit))
 
-    zrows = wrows // 4
+    zrows = wrows // 8
     own_x = [send_w(k, 0, rel, 2) for k in range(3)]
     own_z = [send_w(k, 1, rel, 4) for k in range(3)]
     own_c = [send_w(k, 2, rel, 1) for k in range(3)]
@@ -393,9 +393,7 @@
     grad_start, grad_finish = swap(
         lambda p: grad_out.at[block(p), :], grad_in.at[block(me), :], grad_s, grad_r
     )
-    grad_start()
     own_z[2].start()
-    grad_in[block(me), :] = grad_out[block(me), :]
 
     def squares(q):
         def add(j, total):
@@ -439,6 +437,9 @@
     for k in range(3):
         if k:
             pass_on(k)
+            if k == 1:
+                grad_start()
+                grad_in[block(me), :] = grad_out[block(me), :]
             pass_diag(k)
         own_c[k].wait_recv()
         x_core[k].wait_recv()

time: 133 us -> 133 us (level)
  no operation moved by 1% of the time
where the time goes in v6:
time: 133 us
  Pallas kernels  127 us (95%)
  other arithmetic  4.36 us (3%)
  between operations  1.33 us (1%)
    pallas_call x1, Pallas kernels, local_16(): pl.pallas_call(exchange_kernel, out_shape=(jax.ShapeDtypeStruct((tokens,...  127 us
    mul x1, other arithmetic, local_16(): image_grad = gsum * text_rows.astype(jnp.float32)  4.36 us

profile of v6, /device:TPU:0, one launch (start us, length us, event | category | flops | bytes accessed | tf_op | source)
XLA Modules:
  0.0 133.1 jit_solution(5048679001848118638)
XLA Ops:
  1.3 0.0 copy-start
  1.3 0.0 copy-start.1
  1.3 126.7 %shard_map.139 = (bf16[128,1024]{1,0:T(8,128)(2,1)}, f32[256,2048]{1,0:T(8,128)}) custom-call(s32[1]{0:T(128)S(6)} %copy.16.length_ref, s32[128]{0:T(128)} %bitcast.1, s32[128]{0:T(128)} %row_ref.1, f32[256]{0:T(256)} %price_ref.1, bf16[2048]{0:T(1024)(128)(2,1)} %dir_ref.1, bf16[2048]{0:T(1024)(128)(2,1)} %gain_ref.1, bf16[256,2048]{1,0:T(8,128)(2,1)} %text_hbm.1, ...), custom_call_target="tpu_custom_call" | custom-call | tf_op jit(solution)/shard_map/pallas_call | solution.py:537
  128.0 0.0 copy-done
  128.0 0.0 copy-done.1
  128.0 0.0 copy-start.2
  128.0 4.4 %convert_multiply_fusion = (f32[256,2048]{1,0:T(8,128)}, f32[256,2048]{1,0:T(8,128)}) fusion(f32[256,2048]{1,0:T(8,128)} %get-tuple-element.6, bf16[256,2048]{1,0:T(8,128)(2,1)S(1)} %copy-done, bf16[256,2048]{1,0:T(8,128)(2,1)S(1)} %copy-done.1), kind=kLoop, calls=%fused_computation | loop fusion | flops 2097152 | bytes 8388608 | tf_op jit(solution)/shard_map/mul | solution.py:579
  132.4 0.0 copy-done.2
  132.4 0.7 copy.17
Async XLA Ops:
  1.3 126.7 %copy-start = (bf16[256,2048]{1,0:T(8,128)(2,1)S(1)}, bf16[256,2048]{1,0:T(8,128)(2,1)}, u32[]{:S(2)}) copy-start(bf16[256,2048]{1,0:T(8,128)(2,1)} %text_hbm.1) | copy-start | bytes 3145732
  1.3 126.7 %copy-start.1 = (bf16[256,2048]{1,0:T(8,128)(2,1)S(1)}, bf16[256,2048]{1,0:T(8,128)(2,1)}, u32[]{:S(2)}) copy-start(bf16[256,2048]{1,0:T(8,128)(2,1)} %image_hbm.1) | copy-start | bytes 3145732
  128.0 4.4 %copy-start.2 = (bf16[128,1024]{1,0:T(8,128)(2,1)S(1)}, bf16[128,1024]{1,0:T(8,128)(2,1)}, u32[]{:S(2)}) copy-start(bf16[128,1024]{1,0:T(8,128)(2,1)} %get-tuple-element.12) | copy-start | bytes 786436
